TPU v7x, 768 devices: a whole 4x8x12 slice. The times are simulated.
768 devices in a mesh: ctx: 12 (over z), head: 64 (over x, y, core).
Axes of the slice: x: 4, y: 8, z: 12, core: 2. Of those that a mesh axis runs over, the one named last changes fastest.
Arguments:
- query_rows: bfloat16 [3072, 16384], P('ctx', 'head'), may hold values from -5 to 5
- key_rows: bfloat16 [3072, 1024], P('ctx'), may hold values from -5 to 5
- value_rows: bfloat16 [3072, 1024], P('ctx'), may hold values from -6 to 6
- out_grad: bfloat16 [3072, 16384], P('ctx', 'head'), may hold values from -16 to 16
- span_order: int32 [24], replicated, may hold values from 0 to 23, as said below
Outputs:
- attn_out: bfloat16 [3072, 16384], P('ctx', 'head')
- query_grad: bfloat16 [3072, 16384], P('ctx', 'head')
- key_grad: bfloat16 [3072, 1024], P(('ctx', 'head'))
- value_grad: bfloat16 [3072, 1024], P(('ctx', 'head'))
Inputs may be any that keep to these rules, and one draw needn't show every extreme that they name: `span_order`: each of 0 to 23 appears once, and entries 2d and 2d + 1 add up to 23.
All inputs are finite; a program needn't handle non-finite values.
Results may differ from a plain program's by a relative error of at most 0.025.
Values may be sent and summed in bfloat16 or wider, within the bound.
A program may use at most 32 MiB of HBM per device.

v0:
```python
import math

import jax
import jax.numpy as jnp
from jax import lax
from jax.sharding import PartitionSpec as P

KV_HEADS = 8
HEAD_DIM = 128
GROUP = 16


def joined_along(tiles, dim):
    lengths = list(tiles.shape[1:])
    lengths[dim] *= tiles.shape[0]
    return jnp.moveaxis(tiles, 0, dim).reshape(lengths)


def sent_to_all(array, axis):
    count = lax.axis_size(axis)
    return lax.all_to_all(
        jnp.broadcast_to(array[None], (count, *array.shape)), axis, 0, 0, tiled=True
    )


def gather_directly(array, axis, dim):
    return joined_along(sent_to_all(array, axis), dim)


def sent_together(arrays, axis, dim, along):
    ends, at = ([], 0)
    for a in arrays[:-1]:
        at += a.shape[along]
        ends.append(at)
    both = jnp.concatenate(arrays, axis=along)
    return tuple(jnp.split(gather_directly(both, axis, dim), ends, axis=along))


def per_device(query_rows, key_rows, value_rows, out_grad, span_order):
    n_ctx = lax.axis_size("ctx")
    n_head = lax.axis_size("head")
    tokens = query_rows.shape[0]
    q_heads = query_rows.shape[1] // HEAD_DIM
    span_len = tokens // 2
    seq_len = tokens * n_ctx
    rows_out = tokens // n_head
    replicas = n_head // KV_HEADS
    score_scale = 1.0 / math.sqrt(HEAD_DIM)
    ctx_index = lax.axis_index("ctx")
    head_index = lax.axis_index("head")
    kv_group = head_index * q_heads // GROUP
    key_own = lax.dynamic_slice_in_dim(key_rows, kv_group * HEAD_DIM, HEAD_DIM, 1)
    value_own = lax.dynamic_slice_in_dim(value_rows, kv_group * HEAD_DIM, HEAD_DIM, 1)
    positions = (
        span_order[:, None] * span_len + jnp.arange(span_len, dtype=jnp.int32)[None, :]
    ).reshape(seq_len)
    query_pos = lax.dynamic_slice_in_dim(positions, ctx_index * tokens, tokens)
    queries = query_rows.reshape(tokens, q_heads, HEAD_DIM)
    grads = out_grad.reshape(tokens, q_heads, HEAD_DIM)
    keys_all, values_all = sent_together((key_own, value_own), "ctx", 0, 1)
    scores = (
        jnp.einsum("thd,kd->htk", queries, keys_all, preferred_element_type=jnp.float32)
        * score_scale
    )
    visible = positions[None, None, :] <= query_pos[None, :, None]
    scores = jnp.where(visible, scores, -jnp.inf)
    row_top = jnp.max(scores, axis=2, keepdims=True)
    log_total = row_top + jnp.log(jnp.sum(jnp.exp(scores - row_top), axis=2, keepdims=True))
    probs = jnp.exp(scores - log_total)
    probs_low = probs.astype(jnp.bfloat16)
    attended = jnp.einsum(
        "htk,kd->thd", probs_low, values_all, preferred_element_type=jnp.float32
    ).astype(jnp.bfloat16)
    row_dots = jnp.sum(grads.astype(jnp.float32) * attended.astype(jnp.float32), axis=2)
    prob_grad = jnp.einsum("thd,kd->htk", grads, values_all, preferred_element_type=jnp.float32)
    score_grad = (probs * (prob_grad - row_dots.T[:, :, None])).astype(jnp.bfloat16)
    query_grads = (
        jnp.einsum("htk,kd->thd", score_grad, keys_all, preferred_element_type=jnp.float32)
        * score_scale
    ).astype(jnp.bfloat16)
    key_part = (
        jnp.einsum("htk,thd->kd", score_grad, queries, preferred_element_type=jnp.float32)
        * score_scale
    )
    value_part = jnp.einsum("htk,thd->kd", probs_low, grads, preferred_element_type=jnp.float32)
    owned_rows = lax.psum_scatter(
        jnp.concatenate([key_part, value_part], axis=1), "ctx", scatter_dimension=0, tiled=True
    )
    incoming = lax.all_to_all(
        owned_rows.reshape(tokens, 1, 2 * HEAD_DIM), "head", split_axis=0, concat_axis=1, tiled=True
    )
    summed = incoming.reshape(rows_out, KV_HEADS, replicas, 2 * HEAD_DIM).sum(axis=2)
    key_grad = summed[:, :, :HEAD_DIM].reshape(rows_out, KV_HEADS * HEAD_DIM).astype(jnp.bfloat16)
    value_grad = summed[:, :, HEAD_DIM:].reshape(rows_out, KV_HEADS * HEAD_DIM).astype(jnp.bfloat16)
    attn_out = attended.reshape(tokens, q_heads * HEAD_DIM)
    query_grad = query_grads.reshape(tokens, q_heads * HEAD_DIM)
    return (attn_out, query_grad, key_grad, value_grad)


def solution(mesh):
    in_specs = (P("ctx", "head"), P("ctx", None), P("ctx", None), P("ctx", "head"), P())
    out_specs = (
        P("ctx", "head"),
        P("ctx", "head"),
        P(("ctx", "head"), None),
        P(("ctx", "head"), None),
    )
    return jax.shard_map(
        per_device, mesh=mesh, in_specs=in_specs, out_specs=out_specs, check_vma=False
    )
```

profile of v0, /device:TPU:1, one launch (start us, length us, event | category | flops | bytes accessed | tf_op | source)
XLA Modules:
  0.0 184.3 jit_solution(1095976899720467019)
XLA Ops:
  7.2 0.0 copy-start.3
  7.2 0.0 copy-start.4
  7.2 0.0 copy-start.5
  7.2 1.0 constant_dynamic-slice_fusion
  8.2 1.3 broadcast_in_dim.10
  9.5 15.7 %all-to-all-start = ((bf16[12,256,256]{2,1,0:T(8,128)(2,1)}), bf16[12,256,256]{2,1,0:T(8,128)(2,1)S(1)}, u32[]{:S(2)}, u32[]{:S(2)}) async-start(bf16[12,256,256]{2,1,0:T(8,128)(2,1)} %broadcast_in_dim.10), calls=%async_computation | async-start | bytes 3145728 | tf_op jit(solution)/shard_map/all_to_all | solution.py:21
  25.2 0.0 reduce-scatter.2.cloned.1.call-start
  25.3 0.0 copy-done.3
  25.3 0.1 copy.37
  25.4 0.0 copy-done.4
  25.4 0.1 copy.57
  25.5 0.0 copy-done.5
  25.6 0.1 add_bitcast_fusion
  25.6 0.1 dynamic_slice.11
  25.7 1.4 broadcast_compare_fusion
  27.1 51.5 %all-to-all-done = bf16[12,256,256]{2,1,0:T(8,128)(2,1)S(1)} async-done(((bf16[12,256,256]{2,1,0:T(8,128)(2,1)}), bf16[12,256,256]{2,1,0:T(8,128)(2,1)S(1)}, u32[]{:S(2)}, u32[]{:S(2)}) %all-to-all-start) | async-done | bytes 1572896 | tf_op jit(solution)/shard_map/all_to_all | solution.py:21
  78.5 0.0 copy-start
  78.5 1.0 fusion.7
  79.5 0.8 exponential_reduce_fusion
  80.4 0.0 copy-done
  80.4 1.9 %multiply_reduce_fusion = (f32[256,2]{0,1:T(2,128)S(1)}, bf16[128,2,256]{2,0,1:T(8,128)(2,1)}) fusion(bf16[256,256]{0,1:T(8,128)(2,1)S(1)} %copy.37, f32[2,256,3072]{1,2,0:T(8,128)S(1)} %get-tuple-element.19, f32[2,256]{1,0:T(2,128)S(1)} %log_add_fusion, bf16[3072,256]{1,0:T(8,128)(2,1)S(1)} %bitcast.60), kind=kOutput, calls=%fused_computation.18 | convolution fusion | flops 406126080 | bytes 7344128 | tf_op jit(solution)/shard_map/htk,kd->thd/dot_general | solution.py:71
  82.2 0.0 copy-start.1
  82.2 1.2 convolution_bitcast_fusion
  83.4 0.2 copy-done.1
  83.6 1.2 fusion.1
  84.9 1.2 fusion.3
  86.0 2.0 %pad_maximum_fusion = f32[3072,256]{0,1:T(8,128)} fusion(f32[3072,128]{0,1:T(8,128)S(1)} %convolution_bitcast_fusion, f32[3072,128]{0,1:T(8,128)S(1)} %fusion.3), kind=kLoop, calls=%fused_computation.10 | loop fusion | flops 786432 | bytes 6291456 | tf_op jit(solution)/shard_map/concatenate | solution.py:87
  88.0 0.0 copy-start.2
  88.0 0.0 reduce-scatter.2.cloned.1.call-update
  88.1 57.5 %reduce-scatter.2.cloned.1.call-done = f32[256,256]{0,1:T(8,128)} async-done(((f32[3072,256]{0,1:T(8,128)}), f32[256,256]{0,1:T(8,128)}) %reduce-scatter.2.cloned.1.call-update) | async-done | bytes 262160 | tf_op jit(solution)/shard_map/reduce_scatter | solution.py:86
  145.5 1.8 copy.44
  147.3 17.4 %all-to-all-start.1 = ((f32[256,1,256]{2,1,0:T(1,128)}), f32[256,1,256]{2,1,0:T(1,128)S(1)}, u32[]{:S(2)}, u32[]{:S(2)}) async-start(f32[256,1,256]{2,1,0:T(1,128)} %copy.44), calls=%async_computation.2 | async-start | bytes 524288 | tf_op jit(solution)/shard_map/all_to_all | solution.py:89
  164.7 0.0 copy-done.2
  164.7 0.8 copy.45
  165.5 1.7 fusion.4
  167.2 0.8 copy.46
  168.0 8.7 %all-to-all-done.1 = f32[256,1,256]{2,1,0:T(1,128)S(1)} async-done(((f32[256,1,256]{2,1,0:T(1,128)}), f32[256,1,256]{2,1,0:T(1,128)S(1)}, u32[]{:S(2)}, u32[]{:S(2)}) %all-to-all-start.1) | async-done | bytes 262176 | tf_op jit(solution)/shard_map/all_to_all | solution.py:89
  176.7 0.1 copy.56
  176.8 0.6 slice_bitcast_fusion.6
  (4 shorter events, 0.1 us)
Async XLA Ops:
  7.2 18.1 %copy-start.3 = (bf16[256,256]{1,0:T(8,128)(2,1)S(1)}, bf16[256,256]{1,0:T(8,128)(2,1)}, u32[]{:S(2)}) copy-start(bf16[256,256]{1,0:T(8,128)(2,1)} %param.8) | copy-start | bytes 393220
  7.2 18.2 %copy-start.4 = (bf16[256,256]{1,0:T(8,128)(2,1)S(1)}, bf16[256,256]{1,0:T(8,128)(2,1)}, u32[]{:S(2)}) copy-start(bf16[256,256]{1,0:T(8,128)(2,1)} %param.5) | copy-start | bytes 393220
  7.2 18.4 %copy-start.5 = (s32[24]{0:T(128)S(1)}, s32[24]{0:T(128)}, u32[]{:S(2)}) copy-start(s32[24]{0:T(128)} %param.9) | copy-start | bytes 292
  9.5 69.0 %all-to-all-start = ((bf16[12,256,256]{2,1,0:T(8,128)(2,1)}), bf16[12,256,256]{2,1,0:T(8,128)(2,1)S(1)}, u32[]{:S(2)}, u32[]{:S(2)}) async-start(bf16[12,256,256]{2,1,0:T(8,128)(2,1)} %broadcast_in_dim.10), calls=%async_computation | async-start | bytes 3145728 | tf_op jit(solution)/shard_map/all_to_all | solution.py:21
  25.2 120.3 %reduce-scatter.2.cloned.1.call-start = ((), (), s32[]{:S(2)}) async-start(), calls=%async_computation.3 | async-start | bytes 3407872 | tf_op jit(solution)/shard_map/reduce_scatter | solution.py:86
  78.5 1.8 copy-start
  82.2 1.4 copy-start.1
  88.0 76.7 %copy-start.2 = (bf16[128,2,256]{2,0,1:T(8,128)(2,1)S(1)}, bf16[128,2,256]{2,0,1:T(8,128)(2,1)}, u32[]{:S(2)}) copy-start(bf16[128,2,256]{2,0,1:T(8,128)(2,1)} %get-tuple-element.21) | copy-start | bytes 393220
  147.3 29.4 %all-to-all-start.1 = ((f32[256,1,256]{2,1,0:T(1,128)}), f32[256,1,256]{2,1,0:T(1,128)S(1)}, u32[]{:S(2)}, u32[]{:S(2)}) async-start(f32[256,1,256]{2,1,0:T(1,128)} %copy.44), calls=%async_computation.2 | async-start | bytes 524288 | tf_op jit(solution)/shard_map/all_to_all | solution.py:89
Sparse Core Ops, SparseCore 0:
  88.2 57.3 reduce-scatter.1
where the time goes:
time: 185 us; the launch traced here: 184 us
  waiting for transfers between devices  118 us (64%)
  starting transfers between devices  33.1 us (18%)
  between operations  14.2 us (8%)
  matrix products  8.14 us (4%)
  local copies, waits for them, and re-layouts  6.75 us (4%)
  other arithmetic  4.32 us (2%)
    reduce_scatter x1, waiting for transfers between devices, per_device(): lax.psum_scatter(jnp.concatenate([key_part, value_part], axis=1), 'ctx',...  57.5 us
    all_to_all x1, waiting for transfers between devices, sent_to_all(): lax.all_to_all(jnp.broadcast_to(array[None], (count, *array.shape)), axis...  51.5 us
    all_to_all x1, starting transfers between devices, per_device(): lax.all_to_all(owned_rows.reshape(tokens, 1, 2 * HEAD_DIM), 'head', split...  17.4 us
    all_to_all x1, starting transfers between devices, sent_to_all(): lax.all_to_all(jnp.broadcast_to(array[None], (count, *array.shape)), axis...  15.7 us
    all_to_all x1, waiting for transfers between devices, per_device(): lax.all_to_all(owned_rows.reshape(tokens, 1, 2 * HEAD_DIM), 'head', split...  8.72 us
  transfers between devices with their start and end apart: 3, of which 3 were waited for; matrix products, arithmetic and copies ran while one was open for 3% of the time, Pallas kernels for 0%

commit v1 on v0

v1 whole, which is shorter than its diff:
```python
import functools
import math

import jax
import jax.numpy as jnp
from jax import lax
from jax.experimental import pallas as pl
from jax.experimental.pallas import tpu as pltpu
from jax.sharding import PartitionSpec as P

KV_HEADS = 8
HEAD_DIM = 128
SPAN = 128
HIDDEN = -1e30
F32 = jnp.float32
BF16 = jnp.bfloat16
MESH = pl.DeviceIdType.MESH
PLUS, MINUS = 0, 1
KEY, VAL = 0, 1


def dot(a, b):
    return jnp.dot(a, b, preferred_element_type=F32)


def attention_kernel(
    n_ctx,
    order_ref,
    q_hbm,
    k_hbm,
    v_hbm,
    g_hbm,
    o_ref,
    dq_ref,
    dk_ref,
    dv_ref,
    q4,
    g4,
    q_t,
    g_t,
    kv,
    kv_t,
    p_buf,
    dp_buf,
    m_blk,
    stat,
    stat_in,
    pb,
    dsb,
    o_t,
    dq_t,
    o_in,
    dq_in,
    rs_in,
    rs_out,
    y_out,
    y_in,
    f_out,
    f_in,
    load_sem,
    swap_send,
    swap_recv,
    kv_send,
    kv_recv,
    rs_send,
    rs_recv,
    y_send,
    y_recv,
    f_send,
    f_recv,
):
    half = n_ctx // 2
    z = lax.axis_index("ctx")
    head = lax.axis_index("head")
    group = head // 8
    quarter = (head % 8) // 2
    core = head % 2
    sibling = head + 1 - 2 * core
    after = lax.rem(z + 1, n_ctx)
    before = lax.rem(z + n_ctx - 1, n_ctx)
    score_scale = 1.0 / math.sqrt(HEAD_DIM)
    exponent_scale = score_scale * math.log2(math.e)

    rows = pl.ds(pl.multiple_of(core * SPAN, SPAN), SPAN)
    cols = pl.ds(pl.multiple_of(group * HEAD_DIM, HEAD_DIM), HEAD_DIM)
    loads = [
        pltpu.make_async_copy(k_hbm.at[rows, cols], kv.at[KEY, 0, pl.ds(0, SPAN)], load_sem.at[0]),
        pltpu.make_async_copy(v_hbm.at[rows, cols], kv.at[VAL, 0, pl.ds(0, SPAN)], load_sem.at[1]),
    ]
    for h in range(2):
        part = pl.ds(h * HEAD_DIM, HEAD_DIM)
        loads.append(pltpu.make_async_copy(q_hbm.at[:, part], q4.at[0, pl.ds(h * 256, 256)], load_sem.at[2 + h]))
        loads.append(pltpu.make_async_copy(g_hbm.at[:, part], g4.at[0, pl.ds(h * 256, 256)], load_sem.at[4 + h]))
    for load in loads:
        load.start()

    barrier = pltpu.get_barrier_semaphore()

    def greet(ctx_id, head_id):
        pl.semaphore_signal(barrier, inc=1, device_id=(ctx_id, head_id), device_id_type=MESH)

    greet(after, head)
    greet(before, head)
    greet(z, sibling)
    for step in range(1, 4):
        greet(z, group * 8 + 2 * lax.rem(quarter + step, 4) + core)
    span_of_rows = head // 32
    part_of_rows = lax.rem(head, 32) // 8
    own_chunk = group == core * 4 + quarter
    for g in range(KV_HEADS):

        @pl.when(jnp.logical_not(jnp.logical_and(own_chunk, group == g)))
        def _():
            greet(z, g * 8 + 2 * part_of_rows + span_of_rows)

    def remote(src, dst, send, recv, ctx_id, head_id):
        return pltpu.make_async_remote_copy(
            src_ref=src,
            dst_ref=dst,
            send_sem=send,
            recv_sem=recv,
            device_id=(ctx_id, head_id),
            device_id_type=MESH,
        )

    def slot(kind, t, side):
        return kv.at[kind, t, pl.ds(side * SPAN, SPAN)]

    def hop(kind, direction, t, last=False):
        if direction == PLUS:
            src = slot(kind, t - 1, 0)
            dst = slot(kind, 0, 1) if last else slot(kind, t, 0)
            to = after
        else:
            src = slot(kind, t - 1, 1)
            if isinstance(t, int) and t == 1:
                src = slot(kind, 0, 0)
            dst = slot(kind, 0, 1) if last else slot(kind, t, 1)
            to = before
        return remote(src, dst, kv_send.at[direction, kind, t - 1], kv_recv.at[direction, kind, t - 1], to, head)

    for load in loads[:2]:
        load.wait()
    self_targets = jnp.where(own_chunk, 1, 0)
    pl.semaphore_wait(barrier, 6 + KV_HEADS - self_targets)
    for kind in (KEY, VAL):
        for direction in (PLUS, MINUS):
            hop(kind, direction, 1).start()
    for load in loads[2:]:
        load.wait()
    swap_q = remote(q4.at[0], q4.at[1], swap_send.at[0], swap_recv.at[0], z, sibling)
    swap_g = remote(g4.at[0], g4.at[1], swap_send.at[1], swap_recv.at[1], z, sibling)
    swap_q.start()
    swap_g.start()

    stat[0:1, :] = jnp.full((1, 1024), HIDDEN, F32)
    stat[1:8, :] = jnp.zeros((7, 1024), F32)
    o_t[...] = jnp.zeros_like(o_t)
    dq_t[...] = jnp.zeros_like(dq_t)
    rs_in[PLUS, VAL, half - 1] = jnp.zeros((SPAN, HEAD_DIM), BF16)
    rs_in[MINUS, KEY, half - 1] = jnp.zeros((SPAN, HEAD_DIM), BF16)

    def turn(side):
        for h in range(2):
            q_t[:, side * 512 + h * 256 : side * 512 + (h + 1) * 256] = q4[side, h * 256 : (h + 1) * 256, :].T
            g_t[:, side * 512 + h * 256 : side * 512 + (h + 1) * 256] = g4[side, h * 256 : (h + 1) * 256, :].T

    turn(0)
    swap_q.wait_recv()
    swap_g.wait_recv()
    turn(1)

    lane = lax.broadcasted_iota(jnp.int32, (1, 256), 1)
    ahead = lax.broadcasted_iota(jnp.int32, (SPAN, 256), 0) - lax.rem(
        lax.broadcasted_iota(jnp.int32, (SPAN, 256), 1), SPAN
    )
    q_span0 = order_ref[2 * z]
    q_span1 = order_ref[2 * z + 1]

    def forward(t, side, block):
        k_span = order_ref[2 * block + core]
        reach = jnp.where(lane < SPAN, (q_span0 - k_span) * SPAN, (q_span1 - k_span) * SPAN)
        visible = ahead <= reach
        part = pl.ds(side * SPAN, SPAN)
        key = kv[KEY, t, part]
        value = kv[VAL, t, part]
        for h in range(4):
            at = slice(h * 256, (h + 1) * 256)
            s = jnp.where(visible, dot(key, q_t[:, at]) * exponent_scale, HIDDEN)
            top = stat[0:1, at]
            new_top = jnp.maximum(top, jnp.max(s, axis=0, keepdims=True))
            p = jnp.exp2(s - new_top)
            dp = dot(value, g_t[:, at])
            shrink = jnp.exp2(top - new_top)
            stat[1:2, at] = stat[1:2, at] * shrink + jnp.sum(p, axis=0, keepdims=True)
            stat[2:3, at] = stat[2:3, at] * shrink + jnp.sum(p * dp, axis=0, keepdims=True)
            stat[0:1, at] = new_top
            m_blk[t, side, 0:1, at] = new_top
            p_buf[t, part, at] = p
            dp_buf[t, part, at] = dp
        kv_t[KEY, t, :, part] = key.T
        kv_t[VAL, t, :, part] = value.T

    forward(0, 0, z)

    def gather_step(t, carry):
        for kind in (KEY, VAL):
            for direction in (PLUS, MINUS):
                hop(kind, direction, t).wait_recv()

                @pl.when(t < half - 1)
                def _():
                    hop(kind, direction, t + 1).start()

                if (kind == KEY) == (direction == PLUS):

                    @pl.when(t == half - 1)
                    def _():
                        hop(kind, direction, t + 1, last=True).start()

        forward(t, 0, lax.rem(z - t + n_ctx, n_ctx))
        forward(t, 1, lax.rem(z + t, n_ctx))
        return carry

    lax.fori_loop(1, half, gather_step, 0)
    hop(KEY, PLUS, half, last=True).wait_recv()
    hop(VAL, MINUS, half, last=True).wait_recv()
    forward(0, 1, lax.rem(z + half, n_ctx))

    swap_stat = remote(stat, stat_in, swap_send.at[2], swap_recv.at[2], z, sibling)
    swap_stat.start()
    swap_stat.wait()
    for mine in range(2):
        at = slice(mine * 512, (mine + 1) * 512)
        other = slice((1 - mine) * 512, (2 - mine) * 512)
        m_own, l_own, d_own = stat[0:1, at], stat[1:2, at], stat[2:3, at]
        m_sib, l_sib, d_sib = stat_in[0:1, other], stat_in[1:2, other], stat_in[2:3, other]
        top = jnp.maximum(m_own, m_sib)
        w_own, w_sib = jnp.exp2(m_own - top), jnp.exp2(m_sib - top)
        inverse = 1.0 / (l_own * w_own + l_sib * w_sib)
        stat[3:4, at] = top
        stat[4:5, at] = inverse
        stat[5:6, at] = (d_own * w_own + d_sib * w_sib) * inverse

    def probs_of(t, sides):
        for side in sides:
            part = pl.ds(side * SPAN, SPAN)
            for h in range(4):
                at = slice(h * 256, (h + 1) * 256)
                factor = jnp.exp2(m_blk[t, side, 0:1, at] - stat[3:4, at]) * stat[4:5, at]
                p = p_buf[t, part, at] * factor
                pb[part, at] = p.astype(BF16)
                dsb[part, at] = (p * (dp_buf[t, part, at] - stat[5:6, at])).astype(BF16)

    def grads_of(sides):
        part = pl.ds(sides[0] * SPAN, len(sides) * SPAN)
        value_grad = dot(pb[part, 0:512], g4[0]) + dot(pb[part, 512:1024], g4[1])
        key_grad = (dot(dsb[part, 0:512], q4[0]) + dot(dsb[part, 512:1024], q4[1])) * score_scale
        return key_grad, value_grad

    def rows_add(t):
        for side in range(2):
            at = slice(side * 512, (side + 1) * 512)
            o_t[side] += dot(kv_t[VAL, t], pb[:, at])
            dq_t[side] += dot(kv_t[KEY, t], dsb[:, at])

    def pass_on(kind, direction, d):
        return remote(
            rs_out.at[direction, kind, d - 1],
            rs_in.at[direction, kind, d - 1],
            rs_send.at[direction, kind, d - 1],
            rs_recv.at[direction, kind, d - 1],
            after if direction == PLUS else before,
            head,
        )

    probs_of(0, (0, 1))
    key_grad, value_grad = grads_of((0, 1))
    rs_out[PLUS, KEY, half - 1] = key_grad[SPAN:].astype(BF16)
    pass_on(KEY, PLUS, half).start()
    rs_out[MINUS, VAL, half - 1] = value_grad[SPAN:].astype(BF16)
    pass_on(VAL, MINUS, half).start()
    own_key_grad = key_grad[:SPAN]
    own_value_grad = value_grad[:SPAN]
    o_in[0] = own_key_grad
    o_in[1] = own_value_grad
    rows_add(0)

    def reduce_step(i, carry):
        d = half - 1 - i
        probs_of(d, (0, 1))
        key_grad, value_grad = grads_of((0, 1))
        for kind, grad in ((KEY, key_grad), (VAL, value_grad)):
            for direction in (PLUS, MINUS):
                mine = grad[SPAN:] if direction == PLUS else grad[:SPAN]
                if (kind == KEY) == (direction == PLUS):
                    pass_on(kind, direction, d + 1).wait_recv()
                else:

                    @pl.when(d < half - 1)
                    def _():
                        pass_on(kind, direction, d + 1).wait_recv()

                rs_out[direction, kind, d - 1] = (mine + rs_in[direction, kind, d].astype(F32)).astype(BF16)
                pass_on(kind, direction, d).start()
        rows_add(d)
        return carry

    lax.fori_loop(0, half - 1, reduce_step, 0)

    swap_o = remote(o_t.at[1], dq_in.at[0], swap_send.at[3], swap_recv.at[3], z, sibling)
    swap_dq = remote(dq_t.at[1], dq_in.at[1], swap_send.at[4], swap_recv.at[4], z, sibling)
    swap_o.start()
    swap_dq.start()

    for kind in (KEY, VAL):
        for direction in (PLUS, MINUS):
            pass_on(kind, direction, 1).wait_recv()
        total = o_in[kind] + rs_in[PLUS, kind, 0].astype(F32) + rs_in[MINUS, kind, 0].astype(F32)
        o_in[kind] = total
        for q in range(4):
            y_out[q, kind * 32 : (kind + 1) * 32, :] = total[q * 32 : (q + 1) * 32].astype(BF16)

    def to_quarter(step):
        other = lax.rem(quarter + step, 4)
        return remote(
            y_out.at[other], y_in.at[step - 1], y_send.at[step - 1], y_recv.at[step - 1], z, group * 8 + 2 * other + core
        )

    for step in range(1, 4):
        to_quarter(step).start()

    swap_o.wait_recv()
    swap_dq.wait_recv()
    for h in range(2):
        at = slice(h * 256, (h + 1) * 256)
        o_ref[:, h * HEAD_DIM : (h + 1) * HEAD_DIM] = (o_t[0, :, at] + dq_in[0, :, at]).T.astype(BF16)
        dq_ref[:, h * HEAD_DIM : (h + 1) * HEAD_DIM] = ((dq_t[0, :, at] + dq_in[1, :, at]) * score_scale).T.astype(BF16)

    chunk = pl.ds(pl.multiple_of(quarter * 32, 32), 32)
    sums = [o_in[kind, chunk, :] for kind in (KEY, VAL)]
    for step in range(1, 4):
        to_quarter(step).wait_recv()
        sums = [sums[kind] + y_in[step - 1, kind * 32 : (kind + 1) * 32, :].astype(F32) for kind in (KEY, VAL)]
    for n in range(8):
        f_out[n, 0:4, :] = sums[KEY][4 * n : 4 * n + 4]
        f_out[n, 4:8, :] = sums[VAL][4 * n : 4 * n + 4]

    def to_owner(n):
        return remote(f_out.at[n], f_in.at[group], f_send.at[n], f_recv.at[0], z, core * 32 + quarter * 8 + n)

    def to_self(n):
        return pltpu.make_async_copy(f_out.at[n], f_in.at[group], f_recv.at[0])

    for n in range(8):
        here = head == core * 32 + quarter * 8 + n

        @pl.when(here)
        def _():
            to_self(n).start()

        @pl.when(jnp.logical_not(here))
        def _():
            to_owner(n).start()

    swap_q.wait_send()
    swap_g.wait_send()
    swap_o.wait_send()
    swap_dq.wait_send()

    def sent(t, carry):
        for kind in (KEY, VAL):
            for direction in (PLUS, MINUS):
                hop(kind, direction, t).wait_send()
                pass_on(kind, direction, t).wait_send()
        return carry

    lax.fori_loop(1, half, sent, 0)
    hop(KEY, PLUS, half, last=True).wait_send()
    hop(VAL, MINUS, half, last=True).wait_send()
    pass_on(KEY, PLUS, half).wait_send()
    pass_on(VAL, MINUS, half).wait_send()
    for step in range(1, 4):
        to_quarter(step).wait_send()
    for n in range(8):

        @pl.when(jnp.logical_not(head == core * 32 + quarter * 8 + n))
        def _():
            to_owner(n).wait_send()

    pltpu.make_async_copy(f_out, f_in, f_recv.at[0]).wait()
    for g in range(KV_HEADS):
        at = slice(g * HEAD_DIM, (g + 1) * HEAD_DIM)
        dk_ref[:, at] = f_in[g, 0:4, :].astype(BF16)
        dv_ref[:, at] = f_in[g, 4:8, :].astype(BF16)


def per_device(query_rows, key_rows, value_rows, out_grad, span_order):
    n_ctx = lax.axis_size("ctx")
    half = n_ctx // 2
    vmem = pltpu.VMEM
    dma = pltpu.SemaphoreType.DMA
    anywhere = pl.BlockSpec(memory_space=pl.ANY)
    local = pl.BlockSpec(memory_space=pltpu.VMEM)
    return pl.pallas_call(
        functools.partial(attention_kernel, n_ctx),
        out_shape=(
            jax.ShapeDtypeStruct((256, 256), BF16),
            jax.ShapeDtypeStruct((256, 256), BF16),
            jax.ShapeDtypeStruct((4, 1024), BF16),
            jax.ShapeDtypeStruct((4, 1024), BF16),
        ),
        in_specs=[pl.BlockSpec(memory_space=pltpu.SMEM), anywhere, anywhere, anywhere, anywhere],
        out_specs=(local, local, local, local),
        scratch_shapes=[
            vmem((2, 512, 128), BF16),
            vmem((2, 512, 128), BF16),
            vmem((128, 1024), BF16),
            vmem((128, 1024), BF16),
            vmem((2, half, 256, 128), BF16),
            vmem((2, half, 128, 256), BF16),
            vmem((half, 256, 1024), F32),
            vmem((half, 256, 1024), F32),
            vmem((half, 2, 8, 1024), F32),
            vmem((8, 1024), F32),
            vmem((8, 1024), F32),
            vmem((256, 1024), BF16),
            vmem((256, 1024), BF16),
            vmem((2, 128, 512), F32),
            vmem((2, 128, 512), F32),
            vmem((2, 128, 128), F32),
            vmem((2, 128, 512), F32),
            vmem((2, 2, half, 128, 128), BF16),
            vmem((2, 2, half, 128, 128), BF16),
            vmem((4, 64, 128), BF16),
            vmem((3, 64, 128), BF16),
            vmem((8, 8, 128), F32),
            vmem((8, 8, 128), F32),
            dma((6,)),
            dma((5,)),
            dma((5,)),
            dma((2, 2, half)),
            dma((2, 2, half)),
            dma((2, 2, half)),
            dma((2, 2, half)),
            dma((3,)),
            dma((3,)),
            dma((8,)),
            dma((1,)),
        ],
        compiler_params=pltpu.CompilerParams(
            collective_id=0, has_side_effects=True, vmem_limit_bytes=48 * 1024 * 1024
        ),
    )(span_order, query_rows, key_rows, value_rows, out_grad)


def solution(mesh):
    in_specs = (P("ctx", "head"), P("ctx", None), P("ctx", None), P("ctx", "head"), P())
    out_specs = (
        P("ctx", "head"),
        P("ctx", "head"),
        P(("ctx", "head"), None),
        P(("ctx", "head"), None),
    )
    return jax.shard_map(
        per_device, mesh=mesh, in_specs=in_specs, out_specs=out_specs, check_vma=False
    )
```

time: 185 us -> 80.5 us (0.44)
  waiting for transfers between devices: 118 us -> 0 us
  Pallas kernels: 0 us -> 72.5 us
  starting transfers between devices: 33.1 us -> 0 us
  between operations: 14.2 us -> 0.65 us
  matrix products: 8.14 us -> 0 us
  other arithmetic: 4.32 us -> 0 us
    pallas_call x0 -> x1, Pallas kernels: none -> 72.5 us  [per_device(): pl.pallas_call(functools.partial(attention_kernel, n_ctx), out_shape=(jax...]
    all_to_all x2 -> x0, waiting for transfers between devices: 60.2 us -> none  [the longest x1 51.5 us: sent_to_all(): lax.all_to_all(jnp.broadcast_to(array[None], (count, *array.shape)), axis...]
    reduce_scatter x1 -> x0, waiting for transfers between devices: 57.5 us -> none  [per_device(): lax.psum_scatter(jnp.concatenate([key_part, value_part], axis=1), 'ctx',...]
    all_to_all x2 -> x0, starting transfers between devices: 33.1 us -> none  [the longest x1 17.4 us: per_device(): lax.all_to_all(owned_rows.reshape(tokens, 1, 2 * HEAD_DIM), 'head', split...]
    dot_general x6 -> x0, matrix products: 8.14 us -> none  [the longest x1 1.85 us: per_device(): jnp.einsum('htk,kd->thd', probs_low, values_all, preferred_element_type=j...]
    unnamed x16 -> x14, local copies, waits for them, and re-layouts: 1.92 us -> 7.05 us
    concatenate x2 -> x0, other arithmetic: 2 us -> none  [the longest x1 1.98 us: per_device(): jnp.concatenate([key_part, value_part], axis=1)]
    reshape x2 -> x0, local copies, waits for them, and re-layouts: 1.87 us -> none  [the longest x1 1.77 us: per_device(): owned_rows.reshape(tokens, 1, 2 * HEAD_DIM)]
  transfers between devices with their start and end apart: 3 -> 0, of which waited for: 3 -> 0; matrix products, arithmetic and copies ran while one was open for 3% -> 0% of each run, Pallas kernels for 0% -> 0%
where the time goes in v1:
time: 80.5 us; the launch traced here: 80.2 us
  Pallas kernels  72.5 us (90%)
  local copies, waits for them, and re-layouts  7.05 us (9%)
    pallas_call x1, Pallas kernels, per_device(): pl.pallas_call(functools.partial(attention_kernel, n_ctx), out_shape=(jax...  72.5 us
    unnamed x14, local copies, waits for them, and re-layouts  7.05 us

profile of v1, /device:TPU:1, one launch (start us, length us, event | category | flops | bytes accessed | tf_op | source)
XLA Modules:
  0.0 80.2 jit_solution(9687671673773261983)
XLA Ops:
  0.6 0.0 copy-start
  0.6 1.0 %copy-done = bf16[256,1024]{1,0:T(8,128)(2,1)S(1)} copy-done((bf16[256,1024]{1,0:T(8,128)(2,1)S(1)}, bf16[256,1024]{1,0:T(8,128)(2,1)}, u32[]{:S(2)}) %copy-start) | copy-done | bytes 524312
  1.7 0.0 copy-start.1
  1.7 1.0 %copy-done.1 = bf16[256,1024]{1,0:T(8,128)(2,1)S(1)} copy-done((bf16[256,1024]{1,0:T(8,128)(2,1)S(1)}, bf16[256,1024]{1,0:T(8,128)(2,1)}, u32[]{:S(2)}) %copy-start.1) | copy-done | bytes 524312
  2.7 0.0 copy-start.2
  2.7 0.9 %copy-done.2 = bf16[256,256]{1,0:T(8,128)(2,1)S(1)} copy-done((bf16[256,256]{1,0:T(8,128)(2,1)S(1)}, bf16[256,256]{1,0:T(8,128)(2,1)}, u32[]{:S(2)}) %copy-start.2) | copy-done | bytes 131096
  3.6 0.0 copy-start.3
  3.6 0.9 %copy-done.3 = bf16[256,256]{1,0:T(8,128)(2,1)S(1)} copy-done((bf16[256,256]{1,0:T(8,128)(2,1)S(1)}, bf16[256,256]{1,0:T(8,128)(2,1)}, u32[]{:S(2)}) %copy-start.3) | copy-done | bytes 131096
  4.5 0.0 copy-start.4
  4.5 0.7 copy-done.4
  5.2 72.5 %shard_map.84 = (bf16[256,256]{1,0:T(8,128)(2,1)S(1)}, bf16[256,256]{1,0:T(8,128)(2,1)S(1)}, bf16[4,1024]{1,0:T(4,128)(2,1)S(1)}, bf16[4,1024]{1,0:T(4,128)(2,1)S(1)}) custom-call(s32[24]{0:T(128)S(1)} %copy-done.4, bf16[256,256]{1,0:T(8,128)(2,1)S(1)} %copy-done.2, bf16[256,1024]{1,0:T(8,128)(2,1)S(1)} %copy-done, bf16[256,1024]{1,0:T(8,128)(2,1)S(1)} %copy-done.1, ...), custom_call_target="tpu_custom_call" | custom-call | tf_op jit(solution)/shard_map/pallas_call | solution.py:405
  77.7 0.7 copy.13
  78.4 0.7 copy.14
  79.0 0.6 copy.15
  79.6 0.6 copy.16
Async XLA Ops:
  0.6 1.0 %copy-start = (bf16[256,1024]{1,0:T(8,128)(2,1)S(1)}, bf16[256,1024]{1,0:T(8,128)(2,1)}, u32[]{:S(2)}) copy-start(bf16[256,1024]{1,0:T(8,128)(2,1)} %k_hbm.1) | copy-start | bytes 1572868
  1.7 1.0 %copy-start.1 = (bf16[256,1024]{1,0:T(8,128)(2,1)S(1)}, bf16[256,1024]{1,0:T(8,128)(2,1)}, u32[]{:S(2)}) copy-start(bf16[256,1024]{1,0:T(8,128)(2,1)} %v_hbm.1) | copy-start | bytes 1572868
  2.7 0.9 %copy-start.2 = (bf16[256,256]{1,0:T(8,128)(2,1)S(1)}, bf16[256,256]{1,0:T(8,128)(2,1)}, u32[]{:S(2)}) copy-start(bf16[256,256]{1,0:T(8,128)(2,1)} %q_hbm.1) | copy-start | bytes 393220
  3.6 0.9 %copy-start.3 = (bf16[256,256]{1,0:T(8,128)(2,1)S(1)}, bf16[256,256]{1,0:T(8,128)(2,1)}, u32[]{:S(2)}) copy-start(bf16[256,256]{1,0:T(8,128)(2,1)} %g_hbm.1) | copy-start | bytes 393220
  4.5 0.7 copy-start.4

commit v2 on v1

--- a/solution.py
+++ b/solution.py
@@ -76,16 +76,18 @@
     quarter = (head % 8) // 2
     core = head % 2
     sibling = head + 1 - 2 * core
-    after = lax.rem(z + 1, n_ctx)
-    before = lax.rem(z + n_ctx - 1, n_ctx)
+
+    def along(direction, reach):
+        return lax.rem(z + (reach if direction == PLUS else n_ctx - reach), n_ctx)
+
     score_scale = 1.0 / math.sqrt(HEAD_DIM)
     exponent_scale = score_scale * math.log2(math.e)
 
     rows = pl.ds(pl.multiple_of(core * SPAN, SPAN), SPAN)
     cols = pl.ds(pl.multiple_of(group * HEAD_DIM, HEAD_DIM), HEAD_DIM)
     loads = [
-        pltpu.make_async_copy(k_hbm.at[rows, cols], kv.at[KEY, 0, pl.ds(0, SPAN)], load_sem.at[0]),
-        pltpu.make_async_copy(v_hbm.at[rows, cols], kv.at[VAL, 0, pl.ds(0, SPAN)], load_sem.at[1]),
+        pltpu.make_async_copy(k_hbm.at[rows, cols], kv.at[0, 0, KEY], load_sem.at[0]),
+        pltpu.make_async_copy(v_hbm.at[rows, cols], kv.at[0, 0, VAL], load_sem.at[1]),
     ]
     for h in range(2):
         part = pl.ds(h * HEAD_DIM, HEAD_DIM)
@@ -99,8 +101,9 @@
     def greet(ctx_id, head_id):
         pl.semaphore_signal(barrier, inc=1, device_id=(ctx_id, head_id), device_id_type=MESH)
 
-    greet(after, head)
-    greet(before, head)
+    for direction in (PLUS, MINUS):
+        for reach in (1, 2):
+            greet(along(direction, reach), head)
     greet(z, sibling)
     for step in range(1, 4):
         greet(z, group * 8 + 2 * lax.rem(quarter + step, 4) + core)
@@ -123,29 +126,29 @@
             device_id_type=MESH,
         )
 
-    def slot(kind, t, side):
-        return kv.at[kind, t, pl.ds(side * SPAN, SPAN)]
-
-    def hop(kind, direction, t, last=False):
-        if direction == PLUS:
-            src = slot(kind, t - 1, 0)
-            dst = slot(kind, 0, 1) if last else slot(kind, t, 0)
-            to = after
-        else:
-            src = slot(kind, t - 1, 1)
-            if isinstance(t, int) and t == 1:
-                src = slot(kind, 0, 0)
-            dst = slot(kind, 0, 1) if last else slot(kind, t, 1)
-            to = before
-        return remote(src, dst, kv_send.at[direction, kind, t - 1], kv_recv.at[direction, kind, t - 1], to, head)
+    def hop(direction, source, reach):
+        t = source + reach
+        src = kv.at[source, direction if source else 0]
+        dst = kv.at[t % half, direction if t < half else 1]
+        if t == half:
+            kind = KEY if direction == PLUS else VAL
+            src, dst = src.at[kind], dst.at[kind]
+        return remote(src, dst, kv_send.at[direction, t - 1], kv_recv.at[direction, t - 1], along(direction, reach), head)
+
+    def hops(source, action):
+        for reach in (2, 1):
+            for direction in (PLUS, MINUS):
+                getattr(hop(direction, source, reach), action)()
+
+    def arrived(t):
+        for direction in (PLUS, MINUS):
+            hop(direction, (t - 1) // 2 * 2, 1 + (t - 1) % 2).wait_recv()
 
     for load in loads[:2]:
         load.wait()
     self_targets = jnp.where(own_chunk, 1, 0)
-    pl.semaphore_wait(barrier, 6 + KV_HEADS - self_targets)
-    for kind in (KEY, VAL):
-        for direction in (PLUS, MINUS):
-            hop(kind, direction, 1).start()
+    pl.semaphore_wait(barrier, 8 + KV_HEADS - self_targets)
+    hops(0, "start")
     for load in loads[2:]:
         load.wait()
     swap_q = remote(q4.at[0], q4.at[1], swap_send.at[0], swap_recv.at[0], z, sibling)
@@ -157,8 +160,8 @@
     stat[1:8, :] = jnp.zeros((7, 1024), F32)
     o_t[...] = jnp.zeros_like(o_t)
     dq_t[...] = jnp.zeros_like(dq_t)
-    rs_in[PLUS, VAL, half - 1] = jnp.zeros((SPAN, HEAD_DIM), BF16)
-    rs_in[MINUS, KEY, half - 1] = jnp.zeros((SPAN, HEAD_DIM), BF16)
+    rs_in[PLUS, half - 1, VAL] = jnp.zeros((SPAN, HEAD_DIM), BF16)
+    rs_in[MINUS, half - 1, KEY] = jnp.zeros((SPAN, HEAD_DIM), BF16)
 
     def turn(side):
         for h in range(2):
@@ -182,8 +185,8 @@
         reach = jnp.where(lane < SPAN, (q_span0 - k_span) * SPAN, (q_span1 - k_span) * SPAN)
         visible = ahead <= reach
         part = pl.ds(side * SPAN, SPAN)
-        key = kv[KEY, t, part]
-        value = kv[VAL, t, part]
+        key = kv[t, side, KEY]
+        value = kv[t, side, VAL]
         for h in range(4):
             at = slice(h * 256, (h + 1) * 256)
             s = jnp.where(visible, dot(key, q_t[:, at]) * exponent_scale, HIDDEN)
@@ -204,27 +207,24 @@
     forward(0, 0, z)
 
     def gather_step(t, carry):
-        for kind in (KEY, VAL):
-            for direction in (PLUS, MINUS):
-                hop(kind, direction, t).wait_recv()
-
-                @pl.when(t < half - 1)
-                def _():
-                    hop(kind, direction, t + 1).start()
-
-                if (kind == KEY) == (direction == PLUS):
-
-                    @pl.when(t == half - 1)
-                    def _():
-                        hop(kind, direction, t + 1, last=True).start()
+        for far in range(2, half, 2):
+
+            @pl.when(t == far - 1)
+            def _():
+                arrived(far)
+                hops(far, "start")
+                arrived(far - 1)
+
+        @pl.when(t == half - 1)
+        def _():
+            arrived(half - 1)
 
         forward(t, 0, lax.rem(z - t + n_ctx, n_ctx))
         forward(t, 1, lax.rem(z + t, n_ctx))
         return carry
 
     lax.fori_loop(1, half, gather_step, 0)
-    hop(KEY, PLUS, half, last=True).wait_recv()
-    hop(VAL, MINUS, half, last=True).wait_recv()
+    arrived(half)
     forward(0, 1, lax.rem(z + half, n_ctx))
 
     swap_stat = remote(stat, stat_in, swap_send.at[2], swap_recv.at[2], z, sibling)
@@ -264,22 +264,20 @@
             o_t[side] += dot(kv_t[VAL, t], pb[:, at])
             dq_t[side] += dot(kv_t[KEY, t], dsb[:, at])
 
-    def pass_on(kind, direction, d):
-        return remote(
-            rs_out.at[direction, kind, d - 1],
-            rs_in.at[direction, kind, d - 1],
-            rs_send.at[direction, kind, d - 1],
-            rs_recv.at[direction, kind, d - 1],
-            after if direction == PLUS else before,
-            head,
-        )
+    def pass_on(direction, d):
+        src, dst = rs_out.at[direction, d - 1], rs_in.at[direction, d - 1]
+        if isinstance(d, int) and d == half:
+            kind = KEY if direction == PLUS else VAL
+            src, dst = src.at[kind], dst.at[kind]
+        reach = 2 - d % 2
+        return remote(src, dst, rs_send.at[direction, d - 1], rs_recv.at[direction, d - 1], along(direction, reach), head)
 
     probs_of(0, (0, 1))
     key_grad, value_grad = grads_of((0, 1))
-    rs_out[PLUS, KEY, half - 1] = key_grad[SPAN:].astype(BF16)
-    pass_on(KEY, PLUS, half).start()
-    rs_out[MINUS, VAL, half - 1] = value_grad[SPAN:].astype(BF16)
-    pass_on(VAL, MINUS, half).start()
+    rs_out[PLUS, half - 1, KEY] = key_grad[SPAN:].astype(BF16)
+    pass_on(PLUS, half).start()
+    rs_out[MINUS, half - 1, VAL] = value_grad[SPAN:].astype(BF16)
+    pass_on(MINUS, half).start()
     own_key_grad = key_grad[:SPAN]
     own_value_grad = value_grad[:SPAN]
     o_in[0] = own_key_grad
@@ -287,22 +285,31 @@
     rows_add(0)
 
     def reduce_step(i, carry):
-        d = half - 1 - i
+        d = half - 1 - 2 * ((i + 1) // 2) + (i + 1) % 2 - 1 // (i + 1)
         probs_of(d, (0, 1))
-        key_grad, value_grad = grads_of((0, 1))
-        for kind, grad in ((KEY, key_grad), (VAL, value_grad)):
-            for direction in (PLUS, MINUS):
-                mine = grad[SPAN:] if direction == PLUS else grad[:SPAN]
-                if (kind == KEY) == (direction == PLUS):
-                    pass_on(kind, direction, d + 1).wait_recv()
-                else:
-
-                    @pl.when(d < half - 1)
+        grads = grads_of((0, 1))
+        for direction in (PLUS, MINUS):
+            part = slice(SPAN, 2 * SPAN) if direction == PLUS else slice(0, SPAN)
+
+            @pl.when(d % 2 == 1)
+            def _():
+                for kind in (KEY, VAL):
+                    rs_out[direction, d - 1, kind] = grads[kind][part].astype(BF16)
+
+            @pl.when(d % 2 == 0)
+            def _():
+                pass_on(direction, d + 1).wait_recv()
+                for far in range(2, half, 2):
+
+                    @pl.when(d == far)
                     def _():
-                        pass_on(kind, direction, d + 1).wait_recv()
-
-                rs_out[direction, kind, d - 1] = (mine + rs_in[direction, kind, d].astype(F32)).astype(BF16)
-                pass_on(kind, direction, d).start()
+                        pass_on(direction, far + 2).wait_recv()
+
+                for kind in (KEY, VAL):
+                    beyond = rs_in[direction, d, kind].astype(F32) + rs_in[direction, d + 1, kind].astype(F32)
+                    rs_out[direction, d - 1, kind] = (grads[kind][part] + beyond).astype(BF16)
+
+            pass_on(direction, d).start()
         rows_add(d)
         return carry
 
@@ -313,10 +320,14 @@
     swap_o.start()
     swap_dq.start()
 
+    for direction in (PLUS, MINUS):
+        for d in (1, 2):
+            pass_on(direction, d).wait_recv()
     for kind in (KEY, VAL):
+        total = o_in[kind]
         for direction in (PLUS, MINUS):
-            pass_on(kind, direction, 1).wait_recv()
-        total = o_in[kind] + rs_in[PLUS, kind, 0].astype(F32) + rs_in[MINUS, kind, 0].astype(F32)
+            for d in (1, 2):
+                total += rs_in[direction, d - 1, kind].astype(F32)
         o_in[kind] = total
         for q in range(4):
             y_out[q, kind * 32 : (kind + 1) * 32, :] = total[q * 32 : (q + 1) * 32].astype(BF16)
@@ -368,18 +379,11 @@
     swap_o.wait_send()
     swap_dq.wait_send()
 
-    def sent(t, carry):
-        for kind in (KEY, VAL):
-            for direction in (PLUS, MINUS):
-                hop(kind, direction, t).wait_send()
-                pass_on(kind, direction, t).wait_send()
-        return carry
-
-    lax.fori_loop(1, half, sent, 0)
-    hop(KEY, PLUS, half, last=True).wait_send()
-    hop(VAL, MINUS, half, last=True).wait_send()
-    pass_on(KEY, PLUS, half).wait_send()
-    pass_on(VAL, MINUS, half).wait_send()
+    for source in range(0, half, 2):
+        hops(source, "wait_send")
+    for direction in (PLUS, MINUS):
+        for d in range(1, half + 1):
+            pass_on(direction, d).wait_send()
     for step in range(1, 4):
         to_quarter(step).wait_send()
     for n in range(8):
@@ -400,7 +404,7 @@
     half = n_ctx // 2
     vmem = pltpu.VMEM
     dma = pltpu.SemaphoreType.DMA
-    anywhere = pl.BlockSpec(memory_space=pl.ANY)
+    anywhere = pl.BlockSpec(memory_space=pltpu.HBM)
     local = pl.BlockSpec(memory_space=pltpu.VMEM)
     return pl.pallas_call(
         functools.partial(attention_kernel, n_ctx),
@@ -417,7 +421,7 @@
             vmem((2, 512, 128), BF16),
             vmem((128, 1024), BF16),
             vmem((128, 1024), BF16),
-            vmem((2, half, 256, 128), BF16),
+            vmem((half, 2, 2, 128, 128), BF16),
             vmem((2, half, 128, 256), BF16),
             vmem((half, 256, 1024), F32),
             vmem((half, 256, 1024), F32),
@@ -430,8 +434,8 @@
             vmem((2, 128, 512), F32),
             vmem((2, 128, 128), F32),
             vmem((2, 128, 512), F32),
-            vmem((2, 2, half, 128, 128), BF16),
-            vmem((2, 2, half, 128, 128), BF16),
+            vmem((2, half, 2, 128, 128), BF16),
+            vmem((2, half, 2, 128, 128), BF16),
             vmem((4, 64, 128), BF16),
             vmem((3, 64, 128), BF16),
             vmem((8, 8, 128), F32),
@@ -439,17 +443,17 @@
             dma((6,)),
             dma((5,)),
             dma((5,)),
-            dma((2, 2, half)),
-            dma((2, 2, half)),
-            dma((2, 2, half)),
-            dma((2, 2, half)),
+            dma((2, half)),
+            dma((2, half)),
+            dma((2, half)),
+            dma((2, half)),
             dma((3,)),
             dma((3,)),
             dma((8,)),
             dma((1,)),
         ],
         compiler_params=pltpu.CompilerParams(
-            collective_id=0, has_side_effects=True, vmem_limit_bytes=48 * 1024 * 1024
+            collective_id=0, has_side_effects=True, vmem_limit_bytes=62 * 1024 * 1024
         ),
     )(span_order, query_rows, key_rows, value_rows, out_grad)
 

time: 80.5 us -> 68.9 us (0.86)
  Pallas kernels: 72.5 us -> 64.4 us
  local copies, waits for them, and re-layouts: 7.05 us -> 3.6 us
    pallas_call x1, Pallas kernels: 72.5 us -> 64.4 us  [per_device(): pl.pallas_call(functools.partial(attention_kernel, n_ctx), out_shape=(jax...]
    unnamed x14 -> x10, local copies, waits for them, and re-layouts: 7.05 us -> 3.6 us
where the time goes in v2:
time: 68.9 us; the launch traced here: 68.6 us
  Pallas kernels  64.4 us (93%)
  local copies, waits for them, and re-layouts  3.6 us (5%)
    pallas_call x1, Pallas kernels, per_device(): pl.pallas_call(functools.partial(attention_kernel, n_ctx), out_shape=(jax...  64.4 us
    unnamed x10, local copies, waits for them, and re-layouts  3.6 us

profile of v2, /device:TPU:1, one launch (start us, length us, event | category | flops | bytes accessed | tf_op | source)
XLA Modules:
  0.0 68.6 jit_solution(10818347489801662270)
XLA Ops:
  0.6 64.4 %shard_map.84 = (bf16[256,256]{1,0:T(8,128)(2,1)}, bf16[256,256]{1,0:T(8,128)(2,1)}, bf16[4,1024]{1,0:T(4,128)(2,1)}, bf16[4,1024]{1,0:T(4,128)(2,1)}) custom-call(s32[24]{0:T(128)} %order_ref.1, bf16[256,256]{1,0:T(8,128)(2,1)} %q_hbm.1, bf16[256,1024]{1,0:T(8,128)(2,1)} %k_hbm.1, bf16[256,1024]{1,0:T(8,128)(2,1)} %v_hbm.1, bf16[256,256]{1,0:T(8,128)(2,1)} %g_hbm.1), custom_call_target="tpu_custom_call" | custom-call | tf_op jit(solution)/shard_map/pallas_call | solution.py:409
  65.0 0.0 copy-start
  65.0 1.6 %copy.13 = bf16[256,256]{1,0:T(8,128)(2,1)} copy(bf16[256,256]{1,0:T(8,128)(2,1)} %get-tuple-element.8) | data formatting | bytes 262144
  66.6 0.0 copy-done
  66.6 0.0 copy-start.2
  66.6 0.7 copy.14
  67.3 0.0 copy-done.2
  67.3 0.0 copy-start.1
  67.3 0.6 copy.15
  67.9 0.1 copy-done.1
  68.0 0.6 copy.16
Async XLA Ops:
  65.0 1.6 %copy-start = (bf16[256,256]{1,0:T(8,128)(2,1)S(1)}, bf16[256,256]{1,0:T(8,128)(2,1)}, u32[]{:S(2)}) copy-start(bf16[256,256]{1,0:T(8,128)(2,1)} %get-tuple-element.9) | copy-start | bytes 393220
  66.6 0.7 %copy-start.2 = (bf16[4,1024]{1,0:T(4,128)(2,1)S(1)}, bf16[4,1024]{1,0:T(4,128)(2,1)}, u32[]{:S(2)}) copy-start(bf16[4,1024]{1,0:T(4,128)(2,1)} %get-tuple-element.10) | copy-start | bytes 24580
  67.3 0.7 %copy-start.1 = (bf16[4,1024]{1,0:T(4,128)(2,1)S(1)}, bf16[4,1024]{1,0:T(4,128)(2,1)}, u32[]{:S(2)}) copy-start(bf16[4,1024]{1,0:T(4,128)(2,1)} %get-tuple-element.11) | copy-start | bytes 24580

commit v3 on v2

v3 whole, which is shorter than its diff:
```python
import functools
import math

import jax
import jax.numpy as jnp
from jax import lax
from jax.experimental import pallas as pl
from jax.experimental.pallas import tpu as pltpu
from jax.sharding import PartitionSpec as P

HEAD_DIM = 128
SPAN = 128
PIECE = 64
QUADS = 16
HIDDEN = -1e30
F32 = jnp.float32
BF16 = jnp.bfloat16
MESH = pl.DeviceIdType.MESH
PLUS, MINUS = 0, 1
KEY, VAL = 0, 1
SIB, PAIR, DIAG = 1, 2, 3
REACH = 3


def dot(a, b):
    return jnp.dot(a, b, preferred_element_type=F32)


def attention_kernel(
    n_ctx,
    order_ref,
    q_hbm,
    k_hbm,
    v_hbm,
    g_hbm,
    o_ref,
    dq_ref,
    dk_ref,
    dv_ref,
    q8,
    g8,
    q_t,
    g_t,
    kv,
    kv_t,
    p_buf,
    dp_buf,
    m_blk,
    stat,
    stat_in,
    both,
    pb,
    dsb,
    o_t,
    dq_t,
    mid_out,
    mid_in,
    last_out,
    last_in,
    own_grad,
    near_grad,
    rs_in,
    rs_out,
    f_out,
    f_in,
    load_sem,
    swap_send,
    swap_recv,
    kv_send,
    kv_recv,
    rs_send,
    rs_recv,
    f_send,
    f_recv,
):
    half = n_ctx // 2
    z = lax.axis_index("ctx")
    head = lax.axis_index("head")
    group = head // 8
    quad = head // 4
    member = head % 4
    core = head % 2
    chip = member // 2
    sibling = head + 1 - 2 * core
    score_scale = 1.0 / math.sqrt(HEAD_DIM)
    exponent_scale = score_scale * math.log2(math.e)

    def mate(bits):
        other = head
        if bits & SIB:
            other = other + 1 - 2 * core
        if bits & PAIR:
            other = other + 2 - 4 * chip
        return other

    def along(direction, reach):
        return lax.rem(z + (reach if direction == PLUS else n_ctx - reach), n_ctx)

    rows = pl.ds(pl.multiple_of(member * PIECE, PIECE), PIECE)
    cols = pl.ds(pl.multiple_of(group * HEAD_DIM, HEAD_DIM), HEAD_DIM)
    loads = [
        pltpu.make_async_copy(k_hbm.at[rows, cols], kv.at[0, 0, KEY], load_sem.at[0]),
        pltpu.make_async_copy(v_hbm.at[rows, cols], kv.at[0, 0, VAL], load_sem.at[1]),
    ]
    for h in range(2):
        part = pl.ds(h * HEAD_DIM, HEAD_DIM)
        loads.append(pltpu.make_async_copy(q_hbm.at[:, part], q8.at[pl.ds(h * 256, 256)], load_sem.at[2 + h]))
        loads.append(pltpu.make_async_copy(g_hbm.at[:, part], g8.at[pl.ds(h * 256, 256)], load_sem.at[4 + h]))
    for load in loads:
        load.start()

    barrier = pltpu.get_barrier_semaphore()

    def greet(ctx_id, head_id):
        pl.semaphore_signal(barrier, inc=1, device_id=(ctx_id, head_id), device_id_type=MESH)

    for direction in (PLUS, MINUS):
        for reach in range(1, REACH + 1):
            greet(along(direction, reach), head)
    for bits in (SIB, PAIR, DIAG):
        greet(z, mate(bits))
    own_rows = head // 16 == member
    for other in range(QUADS):

        @pl.when(jnp.logical_not(jnp.logical_and(own_rows, quad == other)))
        def _():
            greet(z, other * 4 + head // 16)

    def remote(src, dst, send, recv, ctx_id, head_id):
        return pltpu.make_async_remote_copy(
            src_ref=src,
            dst_ref=dst,
            send_sem=send,
            recv_sem=recv,
            device_id=(ctx_id, head_id),
            device_id_type=MESH,
        )

    def hop(direction, source, reach):
        t = source + reach
        src = kv.at[source, direction if source else 0]
        dst = kv.at[t % half, direction if t < half else 1]
        if t == half:
            kind = KEY if direction == PLUS else VAL
            src, dst = src.at[kind], dst.at[kind]
        return remote(src, dst, kv_send.at[direction, t - 1], kv_recv.at[direction, t - 1], along(direction, reach), head)

    def hops(source, action):
        for reach in range(REACH, 0, -1):
            for direction in (PLUS, MINUS):
                getattr(hop(direction, source, reach), action)()

    def arrived(t):
        for direction in (PLUS, MINUS):
            hop(direction, (t - 1) // REACH * REACH, 1 + (t - 1) % REACH).wait_recv()

    def swap(i, src, dst, bits):
        return remote(src, dst, swap_send.at[i], swap_recv.at[i], z, mate(bits))

    def heads_of(bits):
        return pl.ds(bits * 512, 512)

    q_sib = swap(0, q8.at[heads_of(0)], q8.at[heads_of(SIB)], SIB)
    g_sib = swap(1, g8.at[heads_of(0)], g8.at[heads_of(SIB)], SIB)
    q_pair = swap(2, q8.at[heads_of(0)], q8.at[heads_of(PAIR)], PAIR)
    g_pair = swap(3, g8.at[heads_of(0)], g8.at[heads_of(PAIR)], PAIR)
    q_diag = swap(4, q8.at[heads_of(PAIR)], q8.at[heads_of(DIAG)], SIB)
    g_diag = swap(5, g8.at[heads_of(PAIR)], g8.at[heads_of(DIAG)], SIB)
    stats = [swap(5 + bits, stat, stat_in.at[bits - 1], bits) for bits in (PAIR, DIAG, SIB)]
    mid = swap(9, mid_out, mid_in, SIB)
    last = swap(10, last_out, last_in, PAIR)

    for load in loads[:2]:
        load.wait()
    pl.semaphore_wait(barrier, 2 * REACH + 3 + QUADS - jnp.where(own_rows, 1, 0))
    hops(0, "start")
    for load in loads[2:]:
        load.wait()
    for copy in (q_pair, q_sib, g_pair, g_sib):
        copy.start()

    stat[0:8, :] = jnp.full((8, 256), HIDDEN, F32)
    stat[8:24, :] = jnp.zeros((16, 256), F32)
    rs_in[PLUS, half - 1, VAL] = jnp.zeros((PIECE, HEAD_DIM), BF16)
    rs_in[MINUS, half - 1, KEY] = jnp.zeros((PIECE, HEAD_DIM), BF16)

    def turn(bits):
        for h in range(2):
            at = slice(bits * 512 + h * 256, bits * 512 + (h + 1) * 256)
            q_t[:, at] = q8[at, :].T
            g_t[:, at] = g8[at, :].T

    lane = lax.broadcasted_iota(jnp.int32, (1, 256), 1)
    ahead = (
        lax.rem(lax.broadcasted_iota(jnp.int32, (2 * PIECE, 256), 0), PIECE)
        - lax.rem(lax.broadcasted_iota(jnp.int32, (2 * PIECE, 256), 1), SPAN)
        + core * PIECE
    )
    q_span0 = order_ref[2 * z]
    q_span1 = order_ref[2 * z + 1]

    def forward(t, members):
        def reach_of(block):
            k_span = order_ref[2 * lax.rem(block, n_ctx) + chip]
            reach = jnp.where(lane < SPAN, (q_span0 - k_span) * SPAN, (q_span1 - k_span) * SPAN)
            return jnp.broadcast_to(reach, (PIECE, 256))

        reach = jnp.concatenate([reach_of(z + n_ctx - t), reach_of(z + t + half * (1 // (t + 1)))], axis=0)
        visible = ahead <= reach
        key = jnp.concatenate([kv[t, 0, KEY], kv[t, 1, KEY]], axis=0)
        value = jnp.concatenate([kv[t, 0, VAL], kv[t, 1, VAL]], axis=0)
        for row in [2 * bits + h for bits in members for h in range(2)]:
            at = slice(row * 256, (row + 1) * 256)
            top_at, sum_at, dot_at = [slice(8 * i + row, 8 * i + row + 1) for i in range(3)]
            s = jnp.where(visible, dot(key, q_t[:, at]) * exponent_scale, HIDDEN)
            top = stat[top_at, :]
            new_top = jnp.maximum(top, jnp.max(s, axis=0, keepdims=True))
            p = jnp.exp2(s - new_top)
            dp = dot(value, g_t[:, at])
            shrink = jnp.exp2(top - new_top)
            stat[sum_at, :] = stat[sum_at, :] * shrink + jnp.sum(p, axis=0, keepdims=True)
            stat[dot_at, :] = stat[dot_at, :] * shrink + jnp.sum(p * dp, axis=0, keepdims=True)
            stat[top_at, :] = new_top
            m_blk[t, row : row + 1, :] = new_top
            p_buf[t, :, at] = p
            dp_buf[t, :, at] = dp
        if 0 in members:
            kv_t[KEY, t] = key.T
            kv_t[VAL, t] = value.T

    turn(0)
    q_sib.wait_recv()
    g_sib.wait_recv()
    turn(SIB)
    arrived(REACH)
    hops(REACH, "start")
    arrived(1)
    arrived(2)

    def near_pairs(t, carry):
        forward(t, (0, SIB))

        @pl.when(t == 1)
        def _():
            q_pair.wait_recv()
            q_diag.start()

        return carry

    def near_pairs_mate(t, carry):
        forward(t, (PAIR,))
        return carry

    def far_pairs(i, carry):
        forward((REACH + 1 + i) % half, (0, SIB, PAIR))
        return carry

    def all_pairs_diag(t, carry):
        forward(t, (DIAG,))
        return carry

    lax.fori_loop(1, REACH + 1, near_pairs, 0)
    g_pair.wait_recv()
    g_diag.start()
    turn(PAIR)
    lax.fori_loop(1, REACH + 1, near_pairs_mate, 0)
    for t in range(REACH + 1, half + 1):
        arrived(t)
    lax.fori_loop(0, half - REACH, far_pairs, 0)
    q_diag.wait_recv()
    g_diag.wait_recv()
    turn(DIAG)
    lax.fori_loop(0, half, all_pairs_diag, 0)

    for copy in stats:
        copy.start()
    o_t[...] = jnp.zeros_like(o_t)
    dq_t[...] = jnp.zeros_like(dq_t)
    for copy in stats:
        copy.wait()

    def seen_by(bits, kind):
        if bits == 0:
            return stat[8 * kind : 8 * kind + 8, :]
        order = [8 * kind + 2 * (own ^ bits) for own in range(4)]
        return jnp.concatenate([stat_in[bits - 1, at : at + 2, :] for at in order], axis=0)

    tops = [seen_by(bits, 0) for bits in range(4)]
    top = jnp.maximum(jnp.maximum(tops[0], tops[1]), jnp.maximum(tops[2], tops[3]))
    weights = [jnp.exp2(one - top) for one in tops]
    total = sum(seen_by(bits, 1) * weights[bits] for bits in range(4))
    inverse = 1.0 / total
    both[0] = top
    both[1] = inverse
    both[2] = sum(seen_by(bits, 2) * weights[bits] for bits in range(4)) * inverse

    def grads_of(t):
        factor = jnp.exp2(m_blk[t] - both[0]) * both[1]
        row_dots = both[2]
        for row in range(8):
            at = slice(row * 256, (row + 1) * 256)
            p = p_buf[t, :, at] * factor[row : row + 1]
            pb[:, at] = p.astype(BF16)
            dsb[:, at] = (p * (dp_buf[t, :, at] - row_dots[row : row + 1])).astype(BF16)
        return dot(dsb[...], q8[...]) * score_scale, dot(pb[...], g8[...])

    def rows_add(t):
        for bits in range(4):
            at = slice(bits * 512, (bits + 1) * 512)
            o_t[bits] += dot(kv_t[VAL, t], pb[:, at])
            dq_t[bits] += dot(kv_t[KEY, t], dsb[:, at])

    def pass_on(direction, d):
        src, dst = rs_out.at[direction, d - 1], rs_in.at[direction, d - 1]
        if isinstance(d, int) and d == half:
            kind = KEY if direction == PLUS else VAL
            src, dst = src.at[kind], dst.at[kind]
        reach = (d - 1) % REACH + 1
        return remote(src, dst, rs_send.at[direction, d - 1], rs_recv.at[direction, d - 1], along(direction, reach), head)

    def side(direction):
        return slice(PIECE, 2 * PIECE) if direction == PLUS else slice(0, PIECE)

    grads = grads_of(0)
    for direction, kind in ((PLUS, KEY), (MINUS, VAL)):
        rs_out[direction, half - 1, kind] = grads[kind][PIECE:].astype(BF16)
        pass_on(direction, half).start()
    for kind in (KEY, VAL):
        own_grad[kind] = grads[kind][:PIECE]
    rows_add(0)

    def reduce_step(i, carry):
        d = half - 1 - i - i // 2
        grads = grads_of(d)
        for direction in (PLUS, MINUS):
            for kind in (KEY, VAL):
                rs_out[direction, d - 1, kind] = grads[kind][side(direction)].astype(BF16)
            pass_on(direction, d).start()
        rows_add(d)
        return carry

    lax.fori_loop(0, half - 2, reduce_step, 0)

    grads = grads_of(REACH)
    for kind in (KEY, VAL):
        near_grad[kind] = grads[kind]
    rows_add(REACH)
    for i, bits in enumerate((SIB, DIAG)):
        mid_out[i, 0] = o_t[bits].astype(BF16)
        mid_out[i, 1] = dq_t[bits].astype(BF16)
    mid.start()
    for direction in (PLUS, MINUS):
        for d in range(REACH + 1, half + 1):
            pass_on(direction, d).wait_recv()
        for kind in (KEY, VAL):
            beyond = sum(rs_in[direction, d - 1, kind].astype(F32) for d in range(REACH + 1, half + 1))
            rs_out[direction, REACH - 1, kind] = (near_grad[kind, side(direction), :] + beyond).astype(BF16)
        pass_on(direction, REACH).start()

    mid.wait_recv()
    last_out[0] = (o_t[PAIR] + mid_in[1, 0].astype(F32)).astype(BF16)
    last_out[1] = (dq_t[PAIR] + mid_in[1, 1].astype(F32)).astype(BF16)
    last.start()

    for direction in (PLUS, MINUS):
        for d in range(1, REACH + 1):
            pass_on(direction, d).wait_recv()
    for kind in (KEY, VAL):
        total = own_grad[kind]
        for direction in (PLUS, MINUS):
            for d in range(1, REACH + 1):
                total += rs_in[direction, d - 1, kind].astype(F32)
        for n in range(QUADS):
            f_out[n, 4 * kind : 4 * kind + 4, :] = total[4 * n : 4 * n + 4]

    def to_owner(n):
        return remote(f_out.at[n], f_in.at[quad], f_send.at[n], f_recv.at[0], z, member * 16 + n)

    for n in range(QUADS):
        here = head == member * 16 + n

        @pl.when(here)
        def _():
            pltpu.make_async_copy(f_out.at[n], f_in.at[quad], f_recv.at[0]).start()

        @pl.when(jnp.logical_not(here))
        def _():
            to_owner(n).start()

    last.wait_recv()
    for h in range(2):
        at = slice(h * 256, (h + 1) * 256)
        cols_h = slice(h * HEAD_DIM, (h + 1) * HEAD_DIM)
        for i, part, out, scale in ((0, o_t, o_ref, 1.0), (1, dq_t, dq_ref, score_scale)):
            rows_sum = part[0, :, at] + mid_in[0, i, :, at].astype(F32) + last_in[i, :, at].astype(F32)
            out[:, cols_h] = (rows_sum * scale).T.astype(BF16)

    for copy in (q_sib, g_sib, q_pair, g_pair, q_diag, g_diag, mid, last):
        copy.wait_send()
    for source in range(0, half, REACH):
        hops(source, "wait_send")
    for direction in (PLUS, MINUS):
        for d in range(1, half + 1):
            pass_on(direction, d).wait_send()
    for n in range(QUADS):

        @pl.when(head != member * 16 + n)
        def _():
            to_owner(n).wait_send()

    pltpu.make_async_copy(f_out, f_in, f_recv.at[0]).wait()
    for g in range(QUADS // 2):
        at = slice(g * HEAD_DIM, (g + 1) * HEAD_DIM)
        summed = f_in[2 * g] + f_in[2 * g + 1]
        dk_ref[:, at] = summed[0:4].astype(BF16)
        dv_ref[:, at] = summed[4:8].astype(BF16)


def per_device(query_rows, key_rows, value_rows, out_grad, span_order):
    n_ctx = lax.axis_size("ctx")
    half = n_ctx // 2
    vmem = pltpu.VMEM
    dma = pltpu.SemaphoreType.DMA
    outside = pl.BlockSpec(memory_space=pltpu.HBM)
    local = pl.BlockSpec(memory_space=pltpu.VMEM)
    return pl.pallas_call(
        functools.partial(attention_kernel, n_ctx),
        out_shape=(
            jax.ShapeDtypeStruct((256, 256), BF16),
            jax.ShapeDtypeStruct((256, 256), BF16),
            jax.ShapeDtypeStruct((4, 1024), BF16),
            jax.ShapeDtypeStruct((4, 1024), BF16),
        ),
        in_specs=[pl.BlockSpec(memory_space=pltpu.SMEM), outside, outside, outside, outside],
        out_specs=(local, local, local, local),
        scratch_shapes=[
            vmem((2048, 128), BF16),
            vmem((2048, 128), BF16),
            vmem((128, 2048), BF16),
            vmem((128, 2048), BF16),
            vmem((half, 2, 2, PIECE, 128), BF16),
            vmem((2, half, 128, 128), BF16),
            vmem((half, 128, 2048), F32),
            vmem((half, 128, 2048), F32),
            vmem((half, 8, 256), F32),
            vmem((24, 256), F32),
            vmem((3, 24, 256), F32),
            vmem((3, 8, 256), F32),
            vmem((128, 2048), BF16),
            vmem((128, 2048), BF16),
            vmem((4, 128, 512), F32),
            vmem((4, 128, 512), F32),
            vmem((2, 2, 128, 512), BF16),
            vmem((2, 2, 128, 512), BF16),
            vmem((2, 128, 512), BF16),
            vmem((2, 128, 512), BF16),
            vmem((2, PIECE, 128), F32),
            vmem((2, 2 * PIECE, 128), F32),
            vmem((2, half, 2, PIECE, 128), BF16),
            vmem((2, half, 2, PIECE, 128), BF16),
            vmem((QUADS, 8, 128), F32),
            vmem((QUADS, 8, 128), F32),
            dma((6,)),
            dma((11,)),
            dma((11,)),
            dma((2, half)),
            dma((2, half)),
            dma((2, half)),
            dma((2, half)),
            dma((QUADS,)),
            dma((1,)),
        ],
        compiler_params=pltpu.CompilerParams(
            collective_id=0, has_side_effects=True, vmem_limit_bytes=62 * 1024 * 1024
        ),
    )(span_order, query_rows, key_rows, value_rows, out_grad)


def solution(mesh):
    in_specs = (P("ctx", "head"), P("ctx", None), P("ctx", None), P("ctx", "head"), P())
    out_specs = (
        P("ctx", "head"),
        P("ctx", "head"),
        P(("ctx", "head"), None),
        P(("ctx", "head"), None),
    )
    return jax.shard_map(
        per_device, mesh=mesh, in_specs=in_specs, out_specs=out_specs, check_vma=False
    )
```

time: 68.9 us -> 60.5 us (0.88)
  Pallas kernels: 64.4 us -> 56 us
    pallas_call x1, Pallas kernels: 64.4 us -> 56 us  [per_device(): pl.pallas_call(functools.partial(attention_kernel, n_ctx), out_shape=(jax...]
where the time goes in v3:
time: 60.5 us; the launch traced here: 60.3 us
  Pallas kernels  56 us (93%)
  local copies, waits for them, and re-layouts  3.6 us (6%)
  between operations  0.65 us (1%)
    pallas_call x1, Pallas kernels, per_device(): pl.pallas_call(functools.partial(attention_kernel, n_ctx), out_shape=(jax...  56 us
    unnamed x10, local copies, waits for them, and re-layouts  3.6 us

profile of v3, /device:TPU:1, one launch (start us, length us, event | category | flops | bytes accessed | tf_op | source)
XLA Modules:
  0.0 60.3 jit_solution(16694001003844543063)
XLA Ops:
  0.6 56.0 %shard_map.84 = (bf16[256,256]{1,0:T(8,128)(2,1)}, bf16[256,256]{1,0:T(8,128)(2,1)}, bf16[4,1024]{1,0:T(4,128)(2,1)}, bf16[4,1024]{1,0:T(4,128)(2,1)}) custom-call(s32[24]{0:T(128)} %order_ref.1, bf16[256,256]{1,0:T(8,128)(2,1)} %q_hbm.1, bf16[256,1024]{1,0:T(8,128)(2,1)} %k_hbm.1, bf16[256,1024]{1,0:T(8,128)(2,1)} %v_hbm.1, bf16[256,256]{1,0:T(8,128)(2,1)} %g_hbm.1), custom_call_target="tpu_custom_call" | custom-call | tf_op jit(solution)/shard_map/pallas_call | solution.py:426
  56.6 0.0 copy-start
  56.6 1.6 %copy.13 = bf16[256,256]{1,0:T(8,128)(2,1)} copy(bf16[256,256]{1,0:T(8,128)(2,1)} %get-tuple-element.8) | data formatting | bytes 262144
  58.3 0.0 copy-done
  58.3 0.0 copy-start.2
  58.3 0.7 %copy.14 = bf16[256,256]{1,0:T(8,128)(2,1)} copy(bf16[256,256]{1,0:T(8,128)(2,1)S(1)} %copy-done) | data formatting | bytes 262144
  58.9 0.0 copy-done.2
  59.0 0.0 copy-start.1
  59.0 0.6 copy.15
  59.6 0.1 copy-done.1
  59.7 0.6 copy.16
Async XLA Ops:
  56.6 1.6 %copy-start = (bf16[256,256]{1,0:T(8,128)(2,1)S(1)}, bf16[256,256]{1,0:T(8,128)(2,1)}, u32[]{:S(2)}) copy-start(bf16[256,256]{1,0:T(8,128)(2,1)} %get-tuple-element.9) | copy-start | bytes 393220
  58.3 0.7 %copy-start.2 = (bf16[4,1024]{1,0:T(4,128)(2,1)S(1)}, bf16[4,1024]{1,0:T(4,128)(2,1)}, u32[]{:S(2)}) copy-start(bf16[4,1024]{1,0:T(4,128)(2,1)} %get-tuple-element.10) | copy-start | bytes 24580
  59.0 0.7 %copy-start.1 = (bf16[4,1024]{1,0:T(4,128)(2,1)S(1)}, bf16[4,1024]{1,0:T(4,128)(2,1)}, u32[]{:S(2)}) copy-start(bf16[4,1024]{1,0:T(4,128)(2,1)} %get-tuple-element.11) | copy-start | bytes 24580

commit v4 on v3

--- a/solution.py
+++ b/solution.py
@@ -33,10 +33,8 @@
     k_hbm,
     v_hbm,
     g_hbm,
-    o_ref,
-    dq_ref,
-    dk_ref,
-    dv_ref,
+    rows_ref,
+    grads_ref,
     q8,
     g8,
     q_t,
@@ -199,6 +197,9 @@
     q_span0 = order_ref[2 * z]
     q_span1 = order_ref[2 * z + 1]
 
+    def span_at(t):
+        return pl.ds(t * SPAN if isinstance(t, int) else pl.multiple_of(t * SPAN, SPAN), SPAN)
+
     def forward(t, members):
         def reach_of(block):
             k_span = order_ref[2 * lax.rem(block, n_ctx) + chip]
@@ -225,8 +226,8 @@
             p_buf[t, :, at] = p
             dp_buf[t, :, at] = dp
         if 0 in members:
-            kv_t[KEY, t] = key.T
-            kv_t[VAL, t] = value.T
+            kv_t[KEY, :, span_at(t)] = key.T
+            kv_t[VAL, :, span_at(t)] = value.T
 
     turn(0)
     q_sib.wait_recv()
@@ -251,12 +252,18 @@
         forward(t, (PAIR,))
         return carry
 
+    def near_pairs_diag(t, carry):
+        forward(t, (DIAG,))
+        return carry
+
     def far_pairs(i, carry):
-        forward((REACH + 1 + i) % half, (0, SIB, PAIR))
-        return carry
-
-    def all_pairs_diag(t, carry):
-        forward(t, (DIAG,))
+        for t in range(REACH + 1, half + 1):
+
+            @pl.when(i == t - REACH - 1)
+            def _():
+                arrived(t)
+
+        forward((REACH + 1 + i) % half, (0, SIB, PAIR, DIAG))
         return carry
 
     lax.fori_loop(1, REACH + 1, near_pairs, 0)
@@ -264,18 +271,14 @@
     g_diag.start()
     turn(PAIR)
     lax.fori_loop(1, REACH + 1, near_pairs_mate, 0)
-    for t in range(REACH + 1, half + 1):
-        arrived(t)
-    lax.fori_loop(0, half - REACH, far_pairs, 0)
     q_diag.wait_recv()
     g_diag.wait_recv()
     turn(DIAG)
-    lax.fori_loop(0, half, all_pairs_diag, 0)
+    lax.fori_loop(1, REACH + 1, near_pairs_diag, 0)
+    lax.fori_loop(0, half - REACH, far_pairs, 0)
 
     for copy in stats:
         copy.start()
-    o_t[...] = jnp.zeros_like(o_t)
-    dq_t[...] = jnp.zeros_like(dq_t)
     for copy in stats:
         copy.wait()
 
@@ -297,18 +300,17 @@
     def grads_of(t):
         factor = jnp.exp2(m_blk[t] - both[0]) * both[1]
         row_dots = both[2]
+        part = span_at(t)
         for row in range(8):
             at = slice(row * 256, (row + 1) * 256)
             p = p_buf[t, :, at] * factor[row : row + 1]
-            pb[:, at] = p.astype(BF16)
-            dsb[:, at] = (p * (dp_buf[t, :, at] - row_dots[row : row + 1])).astype(BF16)
-        return dot(dsb[...], q8[...]) * score_scale, dot(pb[...], g8[...])
-
-    def rows_add(t):
-        for bits in range(4):
-            at = slice(bits * 512, (bits + 1) * 512)
-            o_t[bits] += dot(kv_t[VAL, t], pb[:, at])
-            dq_t[bits] += dot(kv_t[KEY, t], dsb[:, at])
+            pb[part, at] = p.astype(BF16)
+            dsb[part, at] = (p * (dp_buf[t, :, at] - row_dots[row : row + 1])).astype(BF16)
+        return dot(dsb[part, :], q8[...]) * score_scale, dot(pb[part, :], g8[...])
+
+    def rows_of(bits):
+        at = slice(bits * 512, (bits + 1) * 512)
+        return dot(kv_t[VAL], pb[:, at]), dot(kv_t[KEY], dsb[:, at])
 
     def pass_on(direction, d):
         src, dst = rs_out.at[direction, d - 1], rs_in.at[direction, d - 1]
@@ -327,7 +329,6 @@
         pass_on(direction, half).start()
     for kind in (KEY, VAL):
         own_grad[kind] = grads[kind][:PIECE]
-    rows_add(0)
 
     def reduce_step(i, carry):
         d = half - 1 - i - i // 2
@@ -336,7 +337,6 @@
             for kind in (KEY, VAL):
                 rs_out[direction, d - 1, kind] = grads[kind][side(direction)].astype(BF16)
             pass_on(direction, d).start()
-        rows_add(d)
         return carry
 
     lax.fori_loop(0, half - 2, reduce_step, 0)
@@ -344,11 +344,12 @@
     grads = grads_of(REACH)
     for kind in (KEY, VAL):
         near_grad[kind] = grads[kind]
-    rows_add(REACH)
     for i, bits in enumerate((SIB, DIAG)):
-        mid_out[i, 0] = o_t[bits].astype(BF16)
-        mid_out[i, 1] = dq_t[bits].astype(BF16)
+        for j, rows_sum in enumerate(rows_of(bits)):
+            mid_out[i, j] = rows_sum.astype(BF16)
     mid.start()
+    for i, bits in enumerate((0, PAIR)):
+        o_t[i], dq_t[i] = rows_of(bits)
     for direction in (PLUS, MINUS):
         for d in range(REACH + 1, half + 1):
             pass_on(direction, d).wait_recv()
@@ -358,8 +359,8 @@
         pass_on(direction, REACH).start()
 
     mid.wait_recv()
-    last_out[0] = (o_t[PAIR] + mid_in[1, 0].astype(F32)).astype(BF16)
-    last_out[1] = (dq_t[PAIR] + mid_in[1, 1].astype(F32)).astype(BF16)
+    last_out[0] = (o_t[1] + mid_in[1, 0].astype(F32)).astype(BF16)
+    last_out[1] = (dq_t[1] + mid_in[1, 1].astype(F32)).astype(BF16)
     last.start()
 
     for direction in (PLUS, MINUS):
@@ -391,7 +392,7 @@
     for h in range(2):
         at = slice(h * 256, (h + 1) * 256)
         cols_h = slice(h * HEAD_DIM, (h + 1) * HEAD_DIM)
-        for i, part, out, scale in ((0, o_t, o_ref, 1.0), (1, dq_t, dq_ref, score_scale)):
+        for i, part, out, scale in ((0, o_t, rows_ref.at[0], 1.0), (1, dq_t, rows_ref.at[1], score_scale)):
             rows_sum = part[0, :, at] + mid_in[0, i, :, at].astype(F32) + last_in[i, :, at].astype(F32)
             out[:, cols_h] = (rows_sum * scale).T.astype(BF16)
 
@@ -412,8 +413,7 @@
     for g in range(QUADS // 2):
         at = slice(g * HEAD_DIM, (g + 1) * HEAD_DIM)
         summed = f_in[2 * g] + f_in[2 * g + 1]
-        dk_ref[:, at] = summed[0:4].astype(BF16)
-        dv_ref[:, at] = summed[4:8].astype(BF16)
+        grads_ref[:, at] = summed.astype(BF16)
 
 
 def per_device(query_rows, key_rows, value_rows, out_grad, span_order):
@@ -423,33 +423,31 @@
     dma = pltpu.SemaphoreType.DMA
     outside = pl.BlockSpec(memory_space=pltpu.HBM)
     local = pl.BlockSpec(memory_space=pltpu.VMEM)
-    return pl.pallas_call(
+    rows, grads = pl.pallas_call(
         functools.partial(attention_kernel, n_ctx),
         out_shape=(
-            jax.ShapeDtypeStruct((256, 256), BF16),
-            jax.ShapeDtypeStruct((256, 256), BF16),
-            jax.ShapeDtypeStruct((4, 1024), BF16),
-            jax.ShapeDtypeStruct((4, 1024), BF16),
+            jax.ShapeDtypeStruct((2, 256, 256), BF16),
+            jax.ShapeDtypeStruct((8, 1024), BF16),
         ),
         in_specs=[pl.BlockSpec(memory_space=pltpu.SMEM), outside, outside, outside, outside],
-        out_specs=(local, local, local, local),
+        out_specs=(local, local),
         scratch_shapes=[
             vmem((2048, 128), BF16),
             vmem((2048, 128), BF16),
             vmem((128, 2048), BF16),
             vmem((128, 2048), BF16),
             vmem((half, 2, 2, PIECE, 128), BF16),
-            vmem((2, half, 128, 128), BF16),
+            vmem((2, 128, half * 128), BF16),
             vmem((half, 128, 2048), F32),
             vmem((half, 128, 2048), F32),
             vmem((half, 8, 256), F32),
             vmem((24, 256), F32),
             vmem((3, 24, 256), F32),
             vmem((3, 8, 256), F32),
-            vmem((128, 2048), BF16),
-            vmem((128, 2048), BF16),
-            vmem((4, 128, 512), F32),
-            vmem((4, 128, 512), F32),
+            vmem((half * 128, 2048), BF16),
+            vmem((half * 128, 2048), BF16),
+            vmem((2, 128, 512), F32),
+            vmem((2, 128, 512), F32),
             vmem((2, 2, 128, 512), BF16),
             vmem((2, 2, 128, 512), BF16),
             vmem((2, 128, 512), BF16),
@@ -474,6 +472,7 @@
             collective_id=0, has_side_effects=True, vmem_limit_bytes=62 * 1024 * 1024
         ),
     )(span_order, query_rows, key_rows, value_rows, out_grad)
+    return rows[0], rows[1], grads[:4], grads[4:]
 
 
 def solution(mesh):

time: 60.5 us -> 57.2 us (0.945)
  Pallas kernels: 56 us -> 54 us
  local copies, waits for them, and re-layouts: 3.6 us -> 2.3 us
    unnamed x10 -> x2, local copies, waits for them, and re-layouts: 3.6 us -> 0.01 us
    pallas_call x1, Pallas kernels: 56 us -> 54 us  [per_device(): pl.pallas_call(functools.partial(attention_kernel, n_ctx), out_shape=(jax...]
    squeeze x0 -> x1, local copies, waits for them, and re-layouts: none -> 1.69 us  [per_device(): return (rows[0], rows[1], grads[:4], grads[4:])]
    slice x0 -> x1, local copies, waits for them, and re-layouts: none -> 0.61 us  [per_device(): return (rows[0], rows[1], grads[:4], grads[4:])]
where the time goes in v4:
time: 57.2 us; the launch traced here: 57 us
  Pallas kernels  54 us (94%)
  local copies, waits for them, and re-layouts  2.3 us (4%)
  between operations  0.65 us (1%)
    pallas_call x1, Pallas kernels, per_device(): pl.pallas_call(functools.partial(attention_kernel, n_ctx), out_shape=(jax...  54 us
    squeeze x1, local copies, waits for them, and re-layouts, per_device(): return (rows[0], rows[1], grads[:4], grads[4:])  1.69 us

profile of v4, /device:TPU:1, one launch (start us, length us, event | category | flops | bytes accessed | tf_op | source)
XLA Modules:
  0.0 57.0 jit_solution(13587038201751325614)
XLA Ops:
  0.6 54.0 %shard_map.84 = (bf16[2,256,256]{2,1,0:T(8,128)(2,1)}, bf16[8,1024]{1,0:T(8,128)(2,1)}) custom-call(s32[24]{0:T(128)} %order_ref.1, bf16[256,256]{1,0:T(8,128)(2,1)} %q_hbm.1, bf16[256,1024]{1,0:T(8,128)(2,1)} %k_hbm.1, bf16[256,1024]{1,0:T(8,128)(2,1)} %v_hbm.1, bf16[256,256]{1,0:T(8,128)(2,1)} %g_hbm.1), custom_call_target="tpu_custom_call" | custom-call | tf_op jit(solution)/shard_map/pallas_call | solution.py:426
  54.6 0.0 copy-start
  54.7 1.7 %slice_bitcast_fusion = (bf16[256,256]{1,0:T(8,128)(2,1)}, bf16[256,256]{1,0:T(8,128)(2,1)}) fusion(bf16[2,256,256]{2,1,0:T(8,128)(2,1)} %get-tuple-element.6), kind=kLoop, calls=%fused_computation | loop fusion | bytes 524288 | tf_op jit(solution)/shard_map/squeeze | solution.py:475
  56.3 0.0 copy-done
  56.4 0.6 %fusion = (bf16[4,1024]{1,0:T(4,128)(2,1)}, bf16[4,1024]{1,0:T(4,128)(2,1)}) fusion(bf16[8,1024]{1,0:T(8,128)(2,1)S(1)} %copy-done), kind=kLoop, calls=%fused_computation.2 | loop fusion | bytes 32768 | tf_op jit(solution)/shard_map/slice | solution.py:475
Async XLA Ops:
  54.6 1.7 %copy-start = (bf16[8,1024]{1,0:T(8,128)(2,1)S(1)}, bf16[8,1024]{1,0:T(8,128)(2,1)}, u32[]{:S(2)}) copy-start(bf16[8,1024]{1,0:T(8,128)(2,1)} %get-tuple-element.7) | copy-start | bytes 49156

commit v5 on v4

--- a/solution.py
+++ b/solution.py
@@ -39,6 +39,7 @@
     g8,
     q_t,
     g_t,
+    bias,
     kv,
     kv_t,
     p_buf,
@@ -70,6 +71,7 @@
     rs_recv,
     f_send,
     f_recv,
+    word_sem,
 ):
     half = n_ctx // 2
     z = lax.axis_index("ctx")
@@ -117,12 +119,24 @@
             greet(along(direction, reach), head)
     for bits in (SIB, PAIR, DIAG):
         greet(z, mate(bits))
-    own_rows = head // 16 == member
-    for other in range(QUADS):
-
-        @pl.when(jnp.logical_not(jnp.logical_and(own_rows, quad == other)))
-        def _():
-            greet(z, other * 4 + head // 16)
+    column = head // 16
+    place = quad % 4
+    speaks = column == member
+
+    def speaker(step):
+        return column * 16 + lax.rem(place + step, 4) * 4 + member
+
+    @pl.when(speaks)
+    def _():
+        greet(z, speaker(1))
+        greet(z, speaker(3))
+
+    @pl.when(jnp.logical_not(speaks))
+    def _():
+        greet(z, member * 16 + place * 4 + member)
+
+    def word(sem, head_id):
+        pl.semaphore_signal(sem, inc=1, device_id=(z, head_id), device_id_type=MESH)
 
     def remote(src, dst, send, recv, ctx_id, head_id):
         return pltpu.make_async_remote_copy(
@@ -170,12 +184,17 @@
 
     for load in loads[:2]:
         load.wait()
-    pl.semaphore_wait(barrier, 2 * REACH + 3 + QUADS - jnp.where(own_rows, 1, 0))
+    pl.semaphore_wait(barrier, 2 * REACH + 3 + jnp.where(speaks, 5, 0))
     hops(0, "start")
     for load in loads[2:]:
         load.wait()
     for copy in (q_pair, q_sib, g_pair, g_sib):
         copy.start()
+
+    @pl.when(speaks)
+    def _():
+        word(word_sem.at[0], speaker(1))
+        word(word_sem.at[0], speaker(3))
 
     stat[0:8, :] = jnp.full((8, 256), HIDDEN, F32)
     stat[8:24, :] = jnp.zeros((16, 256), F32)
@@ -197,17 +216,19 @@
     q_span0 = order_ref[2 * z]
     q_span1 = order_ref[2 * z + 1]
 
-    def span_at(t):
-        return pl.ds(t * SPAN if isinstance(t, int) else pl.multiple_of(t * SPAN, SPAN), SPAN)
-
-    def forward(t, members):
+    def span_at(place):
+        return pl.ds(place * SPAN if isinstance(place, int) else pl.multiple_of(place * SPAN, SPAN), SPAN)
+
+    def reach_at(t):
         def reach_of(block):
             k_span = order_ref[2 * lax.rem(block, n_ctx) + chip]
             reach = jnp.where(lane < SPAN, (q_span0 - k_span) * SPAN, (q_span1 - k_span) * SPAN)
             return jnp.broadcast_to(reach, (PIECE, 256))
 
-        reach = jnp.concatenate([reach_of(z + n_ctx - t), reach_of(z + t + half * (1 // (t + 1)))], axis=0)
-        visible = ahead <= reach
+        return jnp.concatenate([reach_of(z + n_ctx - t), reach_of(z + t + half * (1 // (t + 1)))], axis=0)
+
+    def forward(t, members, place):
+        visible = ahead <= reach_at(t)
         key = jnp.concatenate([kv[t, 0, KEY], kv[t, 1, KEY]], axis=0)
         value = jnp.concatenate([kv[t, 0, VAL], kv[t, 1, VAL]], axis=0)
         for row in [2 * bits + h for bits in members for h in range(2)]:
@@ -226,8 +247,8 @@
             p_buf[t, :, at] = p
             dp_buf[t, :, at] = dp
         if 0 in members:
-            kv_t[KEY, :, span_at(t)] = key.T
-            kv_t[VAL, :, span_at(t)] = value.T
+            kv_t[KEY, :, span_at(place)] = key.T
+            kv_t[VAL, :, span_at(place)] = value.T
 
     turn(0)
     q_sib.wait_recv()
@@ -239,7 +260,7 @@
     arrived(2)
 
     def near_pairs(t, carry):
-        forward(t, (0, SIB))
+        forward(t, (0, SIB), t)
 
         @pl.when(t == 1)
         def _():
@@ -249,24 +270,53 @@
         return carry
 
     def near_pairs_mate(t, carry):
-        forward(t, (PAIR,))
+        forward(t, (PAIR,), t)
         return carry
 
     def near_pairs_diag(t, carry):
-        forward(t, (DIAG,))
+        forward(t, (DIAG,), t)
         return carry
 
-    def far_pairs(i, carry):
-        for t in range(REACH + 1, half + 1):
-
-            @pl.when(i == t - REACH - 1)
-            def _():
-                arrived(t)
-
-        forward((REACH + 1 + i) % half, (0, SIB, PAIR, DIAG))
-        return carry
+    far = (0, half - 1, half - 2)
+
+    def far_bias():
+        for i, t in enumerate(far):
+            bias[span_at(i), :] = jnp.where(ahead <= reach_at(t), 0.0, HIDDEN)
+
+    def far_pairs():
+        def joined(kind):
+            return jnp.concatenate([kv[t, side, kind] for t in far for side in range(2)], axis=0)
+
+        key, value = joined(KEY), joined(VAL)
+        for row in range(8):
+            at = slice(row * 256, (row + 1) * 256)
+            top_at, sum_at, dot_at = [slice(8 * i + row, 8 * i + row + 1) for i in range(3)]
+            s = dot(key, q_t[:, at]) * exponent_scale + bias[...]
+            top = stat[top_at, :]
+            new_top = jnp.maximum(top, jnp.max(s, axis=0, keepdims=True))
+            p = jnp.exp2(s - new_top)
+            dp = dot(value, g_t[:, at])
+            shrink = jnp.exp2(top - new_top)
+            stat[sum_at, :] = stat[sum_at, :] * shrink + jnp.sum(p, axis=0, keepdims=True)
+            stat[dot_at, :] = stat[dot_at, :] * shrink + jnp.sum(p * dp, axis=0, keepdims=True)
+            stat[top_at, :] = new_top
+            for i, t in enumerate(far):
+                m_blk[t, row : row + 1, :] = new_top
+                p_buf[t, :, at] = p[i * SPAN : (i + 1) * SPAN]
+                dp_buf[t, :, at] = dp[i * SPAN : (i + 1) * SPAN]
+
+    def far_turn():
+        for t in far:
+            for kind in (KEY, VAL):
+                kv_t[kind, :, span_at(t)] = jnp.concatenate([kv[t, 0, kind], kv[t, 1, kind]], axis=0).T
 
     lax.fori_loop(1, REACH + 1, near_pairs, 0)
+
+    @pl.when(speaks)
+    def _():
+        pl.semaphore_wait(word_sem.at[0], 2)
+        word(word_sem.at[1], speaker(1))
+
     g_pair.wait_recv()
     g_diag.start()
     turn(PAIR)
@@ -274,11 +324,22 @@
     q_diag.wait_recv()
     g_diag.wait_recv()
     turn(DIAG)
+
+    @pl.when(speaks)
+    def _():
+        pl.semaphore_wait(word_sem.at[1], 1)
+        for step in range(1, 4):
+            word(word_sem.at[2], lax.rem(column + step, 4) * 16 + place * 4 + member)
+
     lax.fori_loop(1, REACH + 1, near_pairs_diag, 0)
-    lax.fori_loop(0, half - REACH, far_pairs, 0)
+    far_bias()
+    for t in range(REACH + 1, half + 1):
+        arrived(t)
+    far_pairs()
 
     for copy in stats:
         copy.start()
+    far_turn()
     for copy in stats:
         copy.wait()
 
@@ -362,6 +423,10 @@
     last_out[0] = (o_t[1] + mid_in[1, 0].astype(F32)).astype(BF16)
     last_out[1] = (dq_t[1] + mid_in[1, 1].astype(F32)).astype(BF16)
     last.start()
+
+    @pl.when(jnp.logical_not(speaks))
+    def _():
+        pl.semaphore_wait(word_sem.at[2], 1)
 
     for direction in (PLUS, MINUS):
         for d in range(1, REACH + 1):
@@ -436,6 +501,7 @@
             vmem((2048, 128), BF16),
             vmem((128, 2048), BF16),
             vmem((128, 2048), BF16),
+            vmem((3 * SPAN, 256), F32),
             vmem((half, 2, 2, PIECE, 128), BF16),
             vmem((2, 128, half * 128), BF16),
             vmem((half, 128, 2048), F32),
@@ -467,6 +533,7 @@
             dma((2, half)),
             dma((QUADS,)),
             dma((1,)),
+            pltpu.SemaphoreType.REGULAR((3,)),
         ],
         compiler_params=pltpu.CompilerParams(
             collective_id=0, has_side_effects=True, vmem_limit_bytes=62 * 1024 * 1024

time: 57.2 us -> 56.1 us (0.981)
  Pallas kernels: 54 us -> 53 us
    pallas_call x1, Pallas kernels: 54 us -> 53 us  [per_device(): pl.pallas_call(functools.partial(attention_kernel, n_ctx), out_shape=(jax...]
where the time goes in v5:
time: 56.1 us; the launch traced here: 55.9 us
  Pallas kernels  53 us (94%)
  local copies, waits for them, and re-layouts  2.3 us (4%)
  between operations  0.65 us (1%)
    pallas_call x1, Pallas kernels, per_device(): pl.pallas_call(functools.partial(attention_kernel, n_ctx), out_shape=(jax...  53 us
    squeeze x1, local copies, waits for them, and re-layouts, per_device(): return (rows[0], rows[1], grads[:4], grads[4:])  1.69 us

profile of v5, /device:TPU:1, one launch (start us, length us, event | category | flops | bytes accessed | tf_op | source)
XLA Modules:
  0.0 55.9 jit_solution(275829879183465995)
XLA Ops:
  0.6 53.0 %shard_map.84 = (bf16[2,256,256]{2,1,0:T(8,128)(2,1)}, bf16[8,1024]{1,0:T(8,128)(2,1)}) custom-call(s32[24]{0:T(128)} %order_ref.1, bf16[256,256]{1,0:T(8,128)(2,1)} %q_hbm.1, bf16[256,1024]{1,0:T(8,128)(2,1)} %k_hbm.1, bf16[256,1024]{1,0:T(8,128)(2,1)} %v_hbm.1, bf16[256,256]{1,0:T(8,128)(2,1)} %g_hbm.1), custom_call_target="tpu_custom_call" | custom-call | tf_op jit(solution)/shard_map/pallas_call | solution.py:491
  53.6 0.0 copy-start
  53.6 1.7 %slice_bitcast_fusion = (bf16[256,256]{1,0:T(8,128)(2,1)}, bf16[256,256]{1,0:T(8,128)(2,1)}) fusion(bf16[2,256,256]{2,1,0:T(8,128)(2,1)} %get-tuple-element.6), kind=kLoop, calls=%fused_computation | loop fusion | bytes 524288 | tf_op jit(solution)/shard_map/squeeze | solution.py:542
  55.3 0.0 copy-done
  55.3 0.6 %fusion = (bf16[4,1024]{1,0:T(4,128)(2,1)}, bf16[4,1024]{1,0:T(4,128)(2,1)}) fusion(bf16[8,1024]{1,0:T(8,128)(2,1)S(1)} %copy-done), kind=kLoop, calls=%fused_computation.2 | loop fusion | bytes 32768 | tf_op jit(solution)/shard_map/slice | solution.py:542
Async XLA Ops:
  53.6 1.7 %copy-start = (bf16[8,1024]{1,0:T(8,128)(2,1)S(1)}, bf16[8,1024]{1,0:T(8,128)(2,1)}, u32[]{:S(2)}) copy-start(bf16[8,1024]{1,0:T(8,128)(2,1)} %get-tuple-element.7) | copy-start | bytes 49156

commit v6 on v5

--- a/solution.py
+++ b/solution.py
@@ -114,8 +114,8 @@
     def greet(ctx_id, head_id):
         pl.semaphore_signal(barrier, inc=1, device_id=(ctx_id, head_id), device_id_type=MESH)
 
-    for direction in (PLUS, MINUS):
-        for reach in range(1, REACH + 1):
+    for reach in range(REACH, 0, -1):
+        for direction in (PLUS, MINUS):
             greet(along(direction, reach), head)
     for bits in (SIB, PAIR, DIAG):
         greet(z, mate(bits))
@@ -442,16 +442,26 @@
     def to_owner(n):
         return remote(f_out.at[n], f_in.at[quad], f_send.at[n], f_recv.at[0], z, member * 16 + n)
 
-    for n in range(QUADS):
-        here = head == member * 16 + n
-
-        @pl.when(here)
-        def _():
-            pltpu.make_async_copy(f_out.at[n], f_in.at[quad], f_recv.at[0]).start()
-
-        @pl.when(jnp.logical_not(here))
-        def _():
+    row_of_chips = lax.rem(head, 16) // 2
+    places = [(away, other) for away in (4, 3, 5, 2, 6, 1, 7, 0) for other in range(2)]
+
+    def owner(away, other):
+        return 2 * lax.rem(row_of_chips + away, 8) + other
+
+    for away, other in places:
+        n = owner(away, other)
+        if away:
             to_owner(n).start()
+        else:
+            here = head == member * 16 + n
+
+            @pl.when(here)
+            def _():
+                pltpu.make_async_copy(f_out.at[n], f_in.at[quad], f_recv.at[0]).start()
+
+            @pl.when(jnp.logical_not(here))
+            def _():
+                to_owner(n).start()
 
     last.wait_recv()
     for h in range(2):
@@ -468,11 +478,15 @@
     for direction in (PLUS, MINUS):
         for d in range(1, half + 1):
             pass_on(direction, d).wait_send()
-    for n in range(QUADS):
-
-        @pl.when(head != member * 16 + n)
-        def _():
+    for away, other in places:
+        n = owner(away, other)
+        if away:
             to_owner(n).wait_send()
+        else:
+
+            @pl.when(head != member * 16 + n)
+            def _():
+                to_owner(n).wait_send()
 
     pltpu.make_async_copy(f_out, f_in, f_recv.at[0]).wait()
     for g in range(QUADS // 2):

time: 56.1 us -> 56.3 us (level)
  no operation moved by 1% of the time
where the time goes in v6:
time: 56.3 us; the launch traced here: 56.1 us
  Pallas kernels  53.1 us (94%)
  local copies, waits for them, and re-layouts  2.3 us (4%)
  between operations  0.65 us (1%)
    pallas_call x1, Pallas kernels, per_device(): pl.pallas_call(functools.partial(attention_kernel, n_ctx), out_shape=(jax...  53.1 us
    squeeze x1, local copies, waits for them, and re-layouts, per_device(): return (rows[0], rows[1], grads[:4], grads[4:])  1.69 us

profile of v6, /device:TPU:1, one launch (start us, length us, event | category | flops | bytes accessed | tf_op | source)
XLA Modules:
  0.0 56.1 jit_solution(5153534857575561885)
XLA Ops:
  0.6 53.1 %shard_map.84 = (bf16[2,256,256]{2,1,0:T(8,128)(2,1)}, bf16[8,1024]{1,0:T(8,128)(2,1)}) custom-call(s32[24]{0:T(128)} %order_ref.1, bf16[256,256]{1,0:T(8,128)(2,1)} %q_hbm.1, bf16[256,1024]{1,0:T(8,128)(2,1)} %k_hbm.1, bf16[256,1024]{1,0:T(8,128)(2,1)} %v_hbm.1, bf16[256,256]{1,0:T(8,128)(2,1)} %g_hbm.1), custom_call_target="tpu_custom_call" | custom-call | tf_op jit(solution)/shard_map/pallas_call | solution.py:505
  53.7 0.0 copy-start
  53.8 1.7 %slice_bitcast_fusion = (bf16[256,256]{1,0:T(8,128)(2,1)}, bf16[256,256]{1,0:T(8,128)(2,1)}) fusion(bf16[2,256,256]{2,1,0:T(8,128)(2,1)} %get-tuple-element.6), kind=kLoop, calls=%fused_computation | loop fusion | bytes 524288 | tf_op jit(solution)/shard_map/squeeze | solution.py:556
  55.4 0.0 copy-done
  55.4 0.6 %fusion = (bf16[4,1024]{1,0:T(4,128)(2,1)}, bf16[4,1024]{1,0:T(4,128)(2,1)}) fusion(bf16[8,1024]{1,0:T(8,128)(2,1)S(1)} %copy-done), kind=kLoop, calls=%fused_computation.2 | loop fusion | bytes 32768 | tf_op jit(solution)/shard_map/slice | solution.py:556
Async XLA Ops:
  53.7 1.7 %copy-start = (bf16[8,1024]{1,0:T(8,128)(2,1)S(1)}, bf16[8,1024]{1,0:T(8,128)(2,1)}, u32[]{:S(2)}) copy-start(bf16[8,1024]{1,0:T(8,128)(2,1)} %get-tuple-element.7) | copy-start | bytes 49156

commit v7 on v6

--- a/solution.py
+++ b/solution.py
@@ -409,8 +409,6 @@
         for j, rows_sum in enumerate(rows_of(bits)):
             mid_out[i, j] = rows_sum.astype(BF16)
     mid.start()
-    for i, bits in enumerate((0, PAIR)):
-        o_t[i], dq_t[i] = rows_of(bits)
     for direction in (PLUS, MINUS):
         for d in range(REACH + 1, half + 1):
             pass_on(direction, d).wait_recv()
@@ -419,6 +417,8 @@
             rs_out[direction, REACH - 1, kind] = (near_grad[kind, side(direction), :] + beyond).astype(BF16)
         pass_on(direction, REACH).start()
 
+    for i, bits in enumerate((0, PAIR)):
+        o_t[i], dq_t[i] = rows_of(bits)
     mid.wait_recv()
     last_out[0] = (o_t[1] + mid_in[1, 0].astype(F32)).astype(BF16)
     last_out[1] = (dq_t[1] + mid_in[1, 1].astype(F32)).astype(BF16)

time: 56.3 us -> 56.8 us (level)
  Pallas kernels: 53.1 us -> 53.7 us
    pallas_call x1, Pallas kernels: 53.1 us -> 53.7 us  [per_device(): pl.pallas_call(functools.partial(attention_kernel, n_ctx), out_shape=(jax...]
where the time goes in v7:
time: 56.8 us; the launch traced here: 56.6 us
  Pallas kernels  53.7 us (95%)
  local copies, waits for them, and re-layouts  2.3 us (4%)
  between operations  0.65 us (1%)
    pallas_call x1, Pallas kernels, per_device(): pl.pallas_call(functools.partial(attention_kernel, n_ctx), out_shape=(jax...  53.7 us
    squeeze x1, local copies, waits for them, and re-layouts, per_device(): return (rows[0], rows[1], grads[:4], grads[4:])  1.69 us

profile of v7, /device:TPU:1, one launch (start us, length us, event | category | flops | bytes accessed | tf_op | source)
XLA Modules:
  0.0 56.6 jit_solution(2313962047245408362)
XLA Ops:
  0.6 53.7 %shard_map.84 = (bf16[2,256,256]{2,1,0:T(8,128)(2,1)}, bf16[8,1024]{1,0:T(8,128)(2,1)}) custom-call(s32[24]{0:T(128)} %order_ref.1, bf16[256,256]{1,0:T(8,128)(2,1)} %q_hbm.1, bf16[256,1024]{1,0:T(8,128)(2,1)} %k_hbm.1, bf16[256,1024]{1,0:T(8,128)(2,1)} %v_hbm.1, bf16[256,256]{1,0:T(8,128)(2,1)} %g_hbm.1), custom_call_target="tpu_custom_call" | custom-call | tf_op jit(solution)/shard_map/pallas_call | solution.py:505
  54.3 0.0 copy-start
  54.3 1.7 %slice_bitcast_fusion = (bf16[256,256]{1,0:T(8,128)(2,1)}, bf16[256,256]{1,0:T(8,128)(2,1)}) fusion(bf16[2,256,256]{2,1,0:T(8,128)(2,1)} %get-tuple-element.6), kind=kLoop, calls=%fused_computation | loop fusion | bytes 524288 | tf_op jit(solution)/shard_map/squeeze | solution.py:556
  56.0 0.0 copy-done
  56.0 0.6 %fusion = (bf16[4,1024]{1,0:T(4,128)(2,1)}, bf16[4,1024]{1,0:T(4,128)(2,1)}) fusion(bf16[8,1024]{1,0:T(8,128)(2,1)S(1)} %copy-done), kind=kLoop, calls=%fused_computation.2 | loop fusion | bytes 32768 | tf_op jit(solution)/shard_map/slice | solution.py:556
Async XLA Ops:
  54.3 1.7 %copy-start = (bf16[8,1024]{1,0:T(8,128)(2,1)S(1)}, bf16[8,1024]{1,0:T(8,128)(2,1)}, u32[]{:S(2)}) copy-start(bf16[8,1024]{1,0:T(8,128)(2,1)} %get-tuple-element.7) | copy-start | bytes 49156

commit v8 on v7

--- a/solution.py
+++ b/solution.py
@@ -409,6 +409,7 @@
         for j, rows_sum in enumerate(rows_of(bits)):
             mid_out[i, j] = rows_sum.astype(BF16)
     mid.start()
+    o_t[1], dq_t[1] = rows_of(PAIR)
     for direction in (PLUS, MINUS):
         for d in range(REACH + 1, half + 1):
             pass_on(direction, d).wait_recv()
@@ -417,12 +418,11 @@
             rs_out[direction, REACH - 1, kind] = (near_grad[kind, side(direction), :] + beyond).astype(BF16)
         pass_on(direction, REACH).start()
 
-    for i, bits in enumerate((0, PAIR)):
-        o_t[i], dq_t[i] = rows_of(bits)
     mid.wait_recv()
     last_out[0] = (o_t[1] + mid_in[1, 0].astype(F32)).astype(BF16)
     last_out[1] = (dq_t[1] + mid_in[1, 1].astype(F32)).astype(BF16)
     last.start()
+    o_t[0], dq_t[0] = rows_of(0)
 
     @pl.when(jnp.logical_not(speaks))
     def _():

time: 56.8 us -> 56.3 us (level)
  Pallas kernels: 53.7 us -> 53.1 us
where the time goes in v8:
time: 56.3 us; the launch traced here: 56.1 us
  Pallas kernels  53.1 us (94%)
  local copies, waits for them, and re-layouts  2.3 us (4%)
  between operations  0.65 us (1%)
    pallas_call x1, Pallas kernels, per_device(): pl.pallas_call(functools.partial(attention_kernel, n_ctx), out_shape=(jax...  53.1 us
    squeeze x1, local copies, waits for them, and re-layouts, per_device(): return (rows[0], rows[1], grads[:4], grads[4:])  1.69 us

profile of v8, /device:TPU:1, one launch (start us, length us, event | category | flops | bytes accessed | tf_op | source)
XLA Modules:
  0.0 56.1 jit_solution(4374998708934732115)
XLA Ops:
  0.6 53.1 %shard_map.84 = (bf16[2,256,256]{2,1,0:T(8,128)(2,1)}, bf16[8,1024]{1,0:T(8,128)(2,1)}) custom-call(s32[24]{0:T(128)} %order_ref.1, bf16[256,256]{1,0:T(8,128)(2,1)} %q_hbm.1, bf16[256,1024]{1,0:T(8,128)(2,1)} %k_hbm.1, bf16[256,1024]{1,0:T(8,128)(2,1)} %v_hbm.1, bf16[256,256]{1,0:T(8,128)(2,1)} %g_hbm.1), custom_call_target="tpu_custom_call" | custom-call | tf_op jit(solution)/shard_map/pallas_call | solution.py:505
  53.8 0.0 copy-start
  53.8 1.7 %slice_bitcast_fusion = (bf16[256,256]{1,0:T(8,128)(2,1)}, bf16[256,256]{1,0:T(8,128)(2,1)}) fusion(bf16[2,256,256]{2,1,0:T(8,128)(2,1)} %get-tuple-element.6), kind=kLoop, calls=%fused_computation | loop fusion | bytes 524288 | tf_op jit(solution)/shard_map/squeeze | solution.py:556
  55.5 0.0 copy-done
  55.5 0.6 %fusion = (bf16[4,1024]{1,0:T(4,128)(2,1)}, bf16[4,1024]{1,0:T(4,128)(2,1)}) fusion(bf16[8,1024]{1,0:T(8,128)(2,1)S(1)} %copy-done), kind=kLoop, calls=%fused_computation.2 | loop fusion | bytes 32768 | tf_op jit(solution)/shard_map/slice | solution.py:556
Async XLA Ops:
  53.8 1.7 %copy-start = (bf16[8,1024]{1,0:T(8,128)(2,1)S(1)}, bf16[8,1024]{1,0:T(8,128)(2,1)}, u32[]{:S(2)}) copy-start(bf16[8,1024]{1,0:T(8,128)(2,1)} %get-tuple-element.7) | copy-start | bytes 49156
